TPU v7x, 32 devices: a whole 2x2x4 slice. The times are simulated.
32 devices in a mesh: basin: 8 (over z, y), member: 4 (over x, core).
Axes of the slice: x: 2, y: 2, z: 4, core: 2. Of those that a mesh axis runs over, the one named last changes fastest.
Arguments:
- forcing: bfloat16 [512, 16, 192], P('basin', 'member'), may hold values from -6 to 6
- tile_part: int32 [512, 2], P('basin'), may hold values from 0 to 7, all different within a row; in each aligned block of 64 rows (0 to 63, 64 to 127, ...) at most 32 rows name the same one
- tile_slot: int32 [512, 2], P('basin'), may hold values from 0 to 31
- tile_weight: float32 [512, 2], P('basin'), may hold values from 0.2 to 1
- w_input: bfloat16 [8, 1024], replicated, may hold values from -2 to 2
- w_encoder: bfloat16 [256, 1024], replicated, may hold values from -0.375 to 0.375
- b_encoder: float32 [1024], replicated, may hold values from -3 to 3
- w_decoder: bfloat16 [256, 1024], replicated, may hold values from -0.375 to 0.375
- b_decoder: float32 [1024], replicated, may hold values from -3 to 3
- w_output: bfloat16 [256], replicated, may hold values from -0.75 to 0.75
- celerity: float32 [256], replicated, may hold values from 0.5 to 4
- storage: float32 [256], replicated, may hold values from 0.5 to 2
- initial_flow: float32 [256, 16], P('basin', 'member'), may hold values from 0.5 to 2
- reach_level: int32 [256], replicated, may hold values from 0 to 3
- upstream: int32 [256, 4], replicated, may hold values from -1 to 255, as said below
Outputs:
- discharge: float32 [256, 16, 6], P('basin', 'member')
- ensemble_mean: float32 [256, 6], P('basin')
Inputs may be any that keep to these rules, and one draw needn't show every extreme that they name: `tile_part`: among the tile rows of one index of basin, no partition is named more than 32 times. `upstream`: each entry is -1 or the index of a reach whose level is lower than this reach's level; reaches of level 0 have only -1.
All inputs are finite; a program needn't handle non-finite values.
Results may differ from a plain program's by a relative error of at most 0.0003.
Values may be sent and summed in bfloat16 or wider, within the bound.
No kernel may reach another device: no remote copies, remote signals or barrier semaphores. Data moves between devices by JAX's collectives and lax.ppermute only.
A program may use at most 192 MiB of HBM per device.

v0:
```python
import jax
import jax.numpy as jnp
from jax import lax
from jax.sharding import PartitionSpec as P

FEAT = 8
DEC = 6
TOP = 2
LEVELS = 4
NEWTON = 4


BETA = 0.6


def cell_update(gate_sum, memory_cell):
    unit_count = memory_cell.shape[-1]
    input_gate = jax.nn.sigmoid(gate_sum[:, :unit_count])
    forget_gate = jax.nn.sigmoid(gate_sum[:, unit_count : 2 * unit_count])
    candidate = jnp.tanh(gate_sum[:, 2 * unit_count : 3 * unit_count])
    output_gate = jax.nn.sigmoid(gate_sum[:, 3 * unit_count :])
    memory_cell = forget_gate * memory_cell + input_gate * candidate
    hidden = (output_gate * jnp.tanh(memory_cell)).astype(jnp.bfloat16)
    return (hidden, memory_cell)


def run_lstm(inputs, w_input, w_encoder, b_encoder, w_decoder, b_decoder, w_output):
    row_count = inputs.shape[0]
    unit_count = w_encoder.shape[0]
    hidden = jnp.zeros((row_count, unit_count), jnp.bfloat16)
    memory_cell = jnp.zeros((row_count, unit_count), jnp.float32)

    def encode(state_pair, forcing_hour):
        hidden, memory_cell = state_pair
        gate_sum = jnp.dot(forcing_hour, w_input, preferred_element_type=jnp.float32)
        gate_sum = (
            gate_sum + jnp.dot(hidden, w_encoder, preferred_element_type=jnp.float32) + b_encoder
        )
        return (cell_update(gate_sum, memory_cell), None)

    (hidden, memory_cell), ignored = lax.scan(
        encode, (hidden, memory_cell), jnp.swapaxes(inputs, 0, 1)
    )

    def decode(state_pair, unused):
        hidden, memory_cell = state_pair
        gate_sum = jnp.dot(hidden, w_decoder, preferred_element_type=jnp.float32) + b_decoder
        hidden, memory_cell = cell_update(gate_sum, memory_cell)
        runoff = jax.nn.softplus(jnp.dot(hidden, w_output, preferred_element_type=jnp.float32))
        return ((hidden, memory_cell), runoff)

    ignored, runoff = lax.scan(decode, (hidden, memory_cell), None, length=DEC)
    return jnp.swapaxes(runoff, 0, 1)


def route_level(source, upstream, celerity, storage, lateral, initial):
    padded = jnp.concatenate([source, jnp.zeros((1,) + source.shape[1:], source.dtype)], axis=0)
    up_index = jnp.where(upstream < 0, source.shape[0], upstream)
    inflow = padded[up_index[:, 0]]
    for entry in range(1, up_index.shape[1]):
        inflow = inflow + padded[up_index[:, entry]]
    speed_rate = celerity[:, None]
    store_rate = storage[:, None]
    previous = initial
    series = []
    for hour_index in range(lateral.shape[2]):
        target = (
            speed_rate * inflow[:, :, hour_index]
            + store_rate * previous**BETA
            + lateral[:, :, hour_index]
        )
        current = previous
        for newton_step in range(NEWTON):
            misfit = speed_rate * current + store_rate * current**BETA - target
            slope_value = speed_rate + BETA * store_rate * current ** (BETA - 1.0)
            current = jnp.maximum(current - misfit / slope_value, 0.5 * current)
        series.append(current)
        previous = current
    return jnp.stack(series, axis=2)


def on_device(
    forcing,
    tile_part,
    tile_slot,
    tile_weight,
    w_input,
    w_encoder,
    b_encoder,
    w_decoder,
    b_decoder,
    w_output,
    celerity,
    storage,
    initial_flow,
    reach_level,
    upstream,
):
    tile_local, mem_local, hour_feat = forcing.shape
    part_count = lax.axis_size("basin")
    basin_local = initial_flow.shape[0]
    payload = mem_local * hour_feat
    entries = tile_local * TOP
    capacity = max(2, 2 * entries // part_count)
    weighted = (
        tile_weight[:, :, None] * forcing.reshape(tile_local, 1, payload).astype(jnp.float32)
    ).astype(jnp.bfloat16)
    weighted = weighted.reshape(entries, payload)
    target_part = tile_part.reshape(entries)
    part_hot = (target_part[:, None] == jnp.arange(part_count, dtype=jnp.int32)[None, :]).astype(
        jnp.int32
    )
    rank_in_part = jnp.sum((jnp.cumsum(part_hot, axis=0) - part_hot) * part_hot, axis=1)
    position = target_part * capacity + rank_in_part
    placement = (
        position[None, :] == jnp.arange(part_count * capacity, dtype=jnp.int32)[:, None]
    ).astype(jnp.bfloat16)
    send_rows = jnp.dot(placement, weighted, preferred_element_type=jnp.float32).astype(
        jnp.bfloat16
    )
    slot_plus = (tile_slot.reshape(entries) + 1).astype(jnp.bfloat16)
    send_slots = (
        jnp.dot(placement, slot_plus[:, None], preferred_element_type=jnp.float32)[:, 0] - 1.0
    ).astype(jnp.bfloat16)
    arrived_rows, arrived_slots = (
        lax.all_to_all(send_rows, "basin", split_axis=0, concat_axis=0, tiled=True),
        lax.all_to_all(send_slots, "basin", split_axis=0, concat_axis=0, tiled=True),
    )
    slot_hot = (
        arrived_slots.astype(jnp.float32)[None, :]
        == jnp.arange(basin_local, dtype=jnp.float32)[:, None]
    ).astype(jnp.bfloat16)
    aggregated = jnp.dot(slot_hot, arrived_rows, preferred_element_type=jnp.float32)
    inputs = aggregated.astype(jnp.bfloat16).reshape(basin_local * mem_local, -1, FEAT)
    lateral = run_lstm(inputs, w_input, w_encoder, b_encoder, w_decoder, b_decoder, w_output)
    lateral = lateral.reshape(basin_local, mem_local, DEC)
    first_row = lax.axis_index("basin") * basin_local
    level_local = lax.dynamic_slice_in_dim(reach_level, first_row, basin_local, 0)
    up_local = lax.dynamic_slice_in_dim(upstream, first_row, basin_local, 0)
    speed_local = lax.dynamic_slice_in_dim(celerity, first_row, basin_local, 0)
    store_local = lax.dynamic_slice_in_dim(storage, first_row, basin_local, 0)
    outflow = jnp.zeros_like(lateral)
    gathered = jnp.zeros((reach_level.shape[0], mem_local, DEC), jnp.float32)
    for level_now in range(LEVELS):
        if level_now > 0:
            gathered = lax.all_gather(outflow, "basin", axis=0, tiled=True)
        routed = route_level(gathered, up_local, speed_local, store_local, lateral, initial_flow)
        outflow = jnp.where((level_local == level_now)[:, None, None], routed, outflow)
    member_total = lax.psum(jnp.sum(outflow, axis=1), "member")
    ensemble = member_total / (mem_local * lax.axis_size("member"))
    return (outflow, ensemble)


def solution(mesh):
    placed = (
        P("basin", "member", None),
        P("basin", None),
        P("basin", None),
        P("basin", None),
        P(),
        P(),
        P(),
        P(),
        P(),
        P(),
        P(),
        P(),
        P("basin", "member"),
        P(),
        P(),
    )
    return jax.shard_map(
        on_device,
        mesh=mesh,
        in_specs=placed,
        out_specs=(P("basin", "member", None), P("basin", None)),
        check_vma=False,
    )
```

profile of v0, /device:TPU:0, one launch (start us, length us, event | category | flops | bytes accessed | tf_op | source)
XLA Modules:
  0.0 178.8 jit_solution(4022523838476000497)
XLA Ops:
  0.7 0.7 copy-done.12
  3.1 0.6 copy.129
  3.7 7.3 %all-to-all-start = ((bf16[8,32,1]{1,2,0:T(2,128)(2,1)}), bf16[8,32,1]{1,2,0:T(2,128)(2,1)S(1)}, u32[]{:S(2)}, u32[]{:S(2)}) async-start(bf16[8,32,1]{1,2,0:T(2,128)(2,1)} %copy.129), calls=%async_computation | async-start | bytes 8192 | tf_op jit(solution)/shard_map/all_to_all | solution.py:127
  11.0 0.7 copy-done.9
  11.7 0.7 copy-done.8
  13.3 0.6 gather_fusion.3
  13.9 0.6 gather_fusion.2
  14.5 0.6 gather_fusion.1
  15.1 0.6 gather_fusion
  15.7 1.1 convolution_convert_fusion
  16.9 0.7 copy-done.13
  17.6 6.0 %all-to-all-start.1 = ((bf16[8,32,768]{2,1,0:T(8,128)(2,1)}), bf16[8,32,768]{2,1,0:T(8,128)(2,1)S(1)}, u32[]{:S(2)}, u32[]{:S(2)}) async-start(bf16[8,32,768]{2,1,0:T(8,128)(2,1)} %bitcast.10), calls=%async_computation.1 | async-start | bytes 786432 | tf_op jit(solution)/shard_map/all_to_all | solution.py:126
  25.9 8.8 %all-to-all-done.1 = bf16[8,32,768]{2,1,0:T(8,128)(2,1)S(1)} async-done(((bf16[8,32,768]{2,1,0:T(8,128)(2,1)}), bf16[8,32,768]{2,1,0:T(8,128)(2,1)S(1)}, u32[]{:S(2)}, u32[]{:S(2)}) %all-to-all-start.1) | async-done | bytes 393248 | tf_op jit(solution)/shard_map/all_to_all | solution.py:126
  34.9 0.9 reshape.87
  36.9 16.7 %while.28 = (s32[]{:T(128)}, bf16[128,256]{1,0:T(8,128)(2,1)S(1)}, f32[128,256]{1,0:T(8,128)S(1)}, bf16[24,128,8]{1,2,0:T(8,128)(2,1)S(1)}, bf16[8,1024]{1,0:T(8...) while((s32[]{:T(128)}, bf16[128,256]{1,0:T(8,128)(2,1)S(1)}, ...), condition=%wide.region_3.4_spmd.clone, body=%wide.region_2.3_spmd.clone.sunk | while | flops 69992448 | bytes 3037300 | solution.py:41
  53.6 0.6 copy-done.14
  54.3 3.7 %while.27 = (s32[]{:T(128)}, bf16[128,256]{1,0:T(8,128)(2,1)S(1)}, f32[128,256]{1,0:T(8,128)S(1)}, f32[6,128]{1,0:T(8,128)S(1)}, bf16[256,1024]{1,0:T(8,128)(2,1...) while((s32[]{:T(128)}, bf16[128,256]{1,0:T(8,128)(2,1)S(1)}, ...), condition=%wide.region_5.6_spmd, body=%wide.region_4.5_spmd.sunk | while | flops 67764992 | bytes 2038889 | solution.py:52
  58.5 0.7 copy-done.6
  60.2 31.5 %all_gather.9 = f32[256,4,6]{2,1,0:T(4,128)S(1)} all-gather(f32[32,4,6]{2,1,0:T(4,128)S(1)} %broadcast_select_fusion), channel_id=1, replica_groups=mesh['basin'=8,'member'=4] {'basin'}, dimensions={0}, use_global_device_ids=true | all-gather | bytes 27648 | tf_op jit(solution)/shard_map/all_gather | solution.py:146
  91.7 0.6 gather_fusion.7
  92.4 0.6 gather_fusion.6
  93.0 0.6 gather_fusion.5
  93.6 0.6 gather_fusion.4
  96.1 31.4 %all_gather.10 = f32[256,4,6]{2,1,0:T(4,128)S(1)} all-gather(f32[32,4,6]{2,1,0:T(4,128)S(1)} %broadcast_select_fusion.1), channel_id=1, replica_groups=mesh['basin'=8,'member'=4] {'basin'}, dimensions={0}, use_global_device_ids=true | all-gather | bytes 27648 | tf_op jit(solution)/shard_map/all_gather | solution.py:146
  127.5 0.6 gather_fusion.11
  129.3 0.6 gather_fusion.8
  131.8 31.2 %all_gather.11 = f32[256,4,6]{2,1,0:T(4,128)S(1)} all-gather(f32[32,4,6]{2,1,0:T(4,128)S(1)} %broadcast_select_fusion.2), channel_id=1, replica_groups=mesh['basin'=8,'member'=4] {'basin'}, dimensions={0}, use_global_device_ids=true | all-gather | bytes 27648 | tf_op jit(solution)/shard_map/all_gather | solution.py:146
  163.1 0.6 gather_fusion.15
  163.7 0.6 gather_fusion.14
  167.4 10.1 %psum.7 = f32[32,6]{1,0:T(8,128)S(1)} all-reduce(f32[32,6]{1,0:T(8,128)S(1)} %get-tuple-element.163), channel_id=1, replica_groups=mesh['basin'=8,'member'=4] {'member'}, use_global_device_ids=true, to_apply=%region_7.8 | all-reduce | flops 192 | bytes 1536 | tf_op jit(solution)/shard_map/psum | solution.py:149
  177.5 0.7 copy.166
  178.2 0.7 copy.165
  (240 shorter events, 35.1 us)
Async XLA Ops:
  0.6 0.7 copy-start.12
  1.4 0.7 copy-start.7
  2.6 10.0 %copy-start.3 = (bf16[64,4,192]{2,1,0:T(4,128)(2,1)S(1)}, bf16[64,4,192]{2,1,0:T(4,128)(2,1)}, u32[]{:S(2)}) copy-start(bf16[64,4,192]{2,1,0:T(4,128)(2,1)} %param.19) | copy-start | bytes 294916
  3.7 13.9 %all-to-all-start = ((bf16[8,32,1]{1,2,0:T(2,128)(2,1)}), bf16[8,32,1]{1,2,0:T(2,128)(2,1)S(1)}, u32[]{:S(2)}, u32[]{:S(2)}) async-start(bf16[8,32,1]{1,2,0:T(2,128)(2,1)} %copy.129), calls=%async_computation | async-start | bytes 8192 | tf_op jit(solution)/shard_map/all_to_all | solution.py:127
  11.0 0.7 copy-start.9
  11.7 0.7 copy-start.8
  16.9 0.7 copy-start.13
  17.6 17.1 %all-to-all-start.1 = ((bf16[8,32,768]{2,1,0:T(8,128)(2,1)}), bf16[8,32,768]{2,1,0:T(8,128)(2,1)S(1)}, u32[]{:S(2)}, u32[]{:S(2)}) async-start(bf16[8,32,768]{2,1,0:T(8,128)(2,1)} %bitcast.10), calls=%async_computation.1 | async-start | bytes 786432 | tf_op jit(solution)/shard_map/all_to_all | solution.py:126
  24.4 0.7 copy-start.10
  25.1 0.7 copy-start.11
  35.9 1.0 copy-start
  35.9 1.0 copy-start.2
  35.9 1.0 copy-start.4
  36.9 16.7 %copy-start.1 = (bf16[256,1024]{1,0:T(8,128)(2,1)S(1)}, bf16[256,1024]{1,0:T(8,128)(2,1)}, u32[]{:S(2)}) copy-start(bf16[256,1024]{1,0:T(8,128)(2,1)} %param.26) | copy-start | bytes 1572868
  36.9 16.7 %copy-start.5 = (f32[1024]{0:T(1024)S(1)}, f32[1024]{0:T(1024)}, u32[]{:S(2)}) copy-start(f32[1024]{0:T(1024)} %param.27) | copy-start | bytes 12292
  53.6 0.7 copy-start.14
  58.5 0.7 copy-start.6
where the time goes:
time: 179 us
  blocking collectives  104 us (58%)
  local copies, waits for them, and re-layouts  25.9 us (14%)
  matrix products  15.9 us (9%)
  starting transfers between devices  13.3 us (7%)
  waiting for transfers between devices  8.82 us (5%)
  other arithmetic  8.64 us (5%)
    all_gather x3, blocking collectives, on_device(): gathered = lax.all_gather(outflow, 'basin', axis=0, tiled=True)  94 us
    psum x1, blocking collectives, on_device(): member_total = lax.psum(jnp.sum(outflow, axis=1), 'member')  10.1 us
    all_to_all x1, waiting for transfers between devices, on_device(): lax.all_to_all(send_rows, 'basin', split_axis=0, concat_axis=0, tiled=True)  8.81 us
    unnamed x35, local copies, waits for them, and re-layouts  8.34 us
    gather x12, local copies, waits for them, and re-layouts, route_level(): inflow = inflow + padded[up_index[:, entry]]  7.29 us
    all_to_all x1, starting transfers between devices, on_device(): lax.all_to_all(send_slots, 'basin', split_axis=0, concat_axis=0, tiled=True)  7.28 us
    dot_general x24, matrix products, encode(): jnp.dot(forcing_hour, w_input, preferred_element_type=jnp.float32)  6.59 us
    all_to_all x1, starting transfers between devices, on_device(): lax.all_to_all(send_rows, 'basin', split_axis=0, concat_axis=0, tiled=True)  6 us
  transfers between devices with their start and end apart: 2, of which 1 were waited for; matrix products, arithmetic and copies ran while one was open for 3% of the time, Pallas kernels for 0%

commit v1 on v0

v1 whole, which is shorter than its diff:
```python
import functools

import jax
import jax.numpy as jnp
from jax import lax
from jax.experimental import pallas as pl
from jax.experimental.pallas import tpu as pltpu
from jax.sharding import PartitionSpec as P

FEAT = 8
DEC = 6
TOP = 2
LEVELS = 4
NEWTON = 4
BETA = 0.6
LANES = 128
KERNEL_REACHES = 512

dot = functools.partial(jnp.dot, preferred_element_type=jnp.float32)


def three_pieces(values):
    high = lax.reduce_precision(values, 8, 7)
    rest = values - high
    middle = lax.reduce_precision(rest, 8, 7)
    return [high, middle, rest - middle]


def cell_update(gate_sum, memory_cell):
    units = memory_cell.shape[-1]
    input_gate = 0.5 * jnp.tanh(0.5 * gate_sum[:, :units]) + 0.5
    forget_gate = 0.5 * jnp.tanh(0.5 * gate_sum[:, units : 2 * units]) + 0.5
    candidate = jnp.tanh(gate_sum[:, 2 * units : 3 * units])
    output_gate = 0.5 * jnp.tanh(0.5 * gate_sum[:, 3 * units :]) + 0.5
    memory_cell = forget_gate * memory_cell + input_gate * candidate
    hidden = (output_gate * jnp.tanh(memory_cell)).astype(jnp.bfloat16)
    return hidden, memory_cell


def lstm_kernel(
    shape, arrived, w_input, w_encoder, b_encoder, w_decoder, b_decoder, w_output, out
):
    hour_feat, basin_local, groups, sources = shape
    hours = hour_feat // FEAT
    devices, tile_local, _ = arrived.shape
    rows = out.shape[1]
    units = w_encoder.shape[0]
    half = lax.rem(lax.axis_index("basin"), groups)
    first = half * rows
    extra_at = hour_feat // LANES * LANES
    lane0 = hour_feat - extra_at

    def add_sources(chunk, total):
        block = arrived[pl.ds(chunk * sources, sources)]
        block = block.reshape(sources * tile_local, block.shape[2]).astype(jnp.float32)
        extra = block[:, extra_at : extra_at + LANES]
        across = extra.T
        for entry in range(TOP):
            col = lane0 + 3 * entry
            weight = extra[:, col : col + 1] + extra[:, col + 1 : col + 2] + extra[:, col + 2 : col + 3]
            term = (weight * block).astype(jnp.bfloat16)
            part = lane0 + 3 * TOP + entry
            slot = part + TOP
            basin = across[part : part + 1] * basin_local + across[slot : slot + 1]
            basin = basin.astype(jnp.int32) - first
            row_of = lax.broadcasted_iota(jnp.int32, (rows, sources * tile_local), 0)
            picked = jnp.where(row_of == basin, 1.0, 0.0).astype(jnp.bfloat16)
            total = total + dot(picked, term)
        return total

    total = jnp.zeros((rows, arrived.shape[2]), jnp.float32)
    if devices == sources:
        total = add_sources(0, total)
    else:
        total = lax.fori_loop(0, devices // sources, add_sources, total)
    inputs = total.astype(jnp.bfloat16)

    owners = rows // basin_local
    flow = arrived[pl.ds(half * owners, owners), 0:basin_local, extra_at : extra_at + LANES]
    flow = flow.astype(jnp.float32).reshape(rows, LANES).T
    at = lane0 + 5 * TOP
    flow = flow[at : at + 1] + flow[at + 1 : at + 2] + flow[at + 2 : at + 3]
    out[DEC : DEC + 1, :] = flow
    out[DEC + 1 :, :] = jnp.zeros((out.shape[0] - DEC - 1, rows), jnp.float32)

    hidden = jnp.zeros((rows, units), jnp.bfloat16)
    memory_cell = jnp.zeros((rows, units), jnp.float32)
    for hour in range(hours):
        gate_sum = dot(inputs[:, hour * FEAT : (hour + 1) * FEAT], w_input[...]) + b_encoder[...]
        gate_sum = gate_sum + dot(hidden, w_encoder[...])
        hidden, memory_cell = cell_update(gate_sum, memory_cell)
    for hour in range(DEC):
        gate_sum = dot(hidden, w_decoder[...]) + b_decoder[...]
        hidden, memory_cell = cell_update(gate_sum, memory_cell)
        runoff = lax.dot_general(
            w_output[...], hidden, (((1,), (1,)), ((), ())), preferred_element_type=jnp.float32
        )[0:1]
        runoff = jnp.maximum(runoff, 0.0) + jnp.log(1.0 + jnp.exp(-jnp.abs(runoff)))
        out[hour : hour + 1, :] = runoff


def power(flow):
    return jnp.exp(BETA * jnp.log(flow))


def route_kernel(member_local, basin_local, gathered, upstream, level_row, celerity, storage, discharge, ensemble):
    reaches = level_row.shape[1]
    halves = reaches // LANES
    per_member = halves * 8
    members = gathered.shape[0] // per_member
    levels = jnp.broadcast_to(level_row[...], (members, reaches))
    source = lax.broadcasted_iota(jnp.int32, (reaches, reaches), 0)
    links = jnp.zeros((reaches, reaches), jnp.float32)
    for entry in range(upstream.shape[0]):
        links = links + jnp.where(source == upstream[entry : entry + 1, :], 1.0, 0.0)
    links = links.astype(jnp.bfloat16)
    speed_rate = jnp.broadcast_to(celerity[...], (members, reaches))
    store_rate = jnp.broadcast_to(storage[...], (members, reaches))

    def row(k):
        return jnp.concatenate(
            [gathered[pl.ds(h * 8 + k, members, stride=per_member), :] for h in range(halves)], axis=1
        )

    lateral = [row(k) for k in range(DEC)]
    current = row(DEC)
    powered = power(current)
    series = [jnp.zeros((members, reaches), jnp.float32) for _ in range(DEC)]
    for step in range(DEC + LEVELS - 1):
        target = jnp.zeros((members, reaches), jnp.float32)
        parts, owners = [], []
        for level in range(LEVELS):
            hour = step - level
            if 0 <= hour < DEC:
                target = jnp.where(levels == level, lateral[hour], target)
                if level:
                    flow = series[hour]
                    for _ in range(3):
                        piece = flow.astype(jnp.bfloat16)
                        parts.append(piece)
                        flow = flow - piece.astype(jnp.float32)
                    owners.append(level)
        if parts:
            sums = dot(jnp.concatenate(parts, axis=0), links)
            for i, level in enumerate(owners):
                at = 3 * i * members
                inflow = sums[at : at + members] + sums[at + members : at + 2 * members]
                inflow = inflow + sums[at + 2 * members : at + 3 * members]
                target = jnp.where(levels == level, target + speed_rate * inflow, target)
        target = target + store_rate * powered
        flow, flow_power = current, powered
        for _ in range(NEWTON):
            ratio = (target - (1.0 - BETA) * store_rate * flow_power) / (
                speed_rate * flow + BETA * store_rate * flow_power
            )
            flow = flow * jnp.maximum(ratio, 0.5)
            flow_power = power(flow)
        active = (levels <= step) & (levels > step - DEC)
        current = jnp.where(active, flow, current)
        powered = jnp.where(active, flow_power, powered)
        for level in range(LEVELS):
            hour = step - level
            if 0 <= hour < DEC:
                series[hour] = jnp.where(levels == level, flow, series[hour])
    column = lax.axis_index("basin") * basin_local
    mine = lax.axis_index("member")
    block = column // LANES
    shift = lax.rem(LANES - lax.rem(column, LANES), LANES)
    for hour in range(DEC):
        value = series[hour]
        picked = value[:, 0:LANES]
        for h in range(1, halves):
            picked = jnp.where(block == h, value[:, h * LANES : (h + 1) * LANES], picked)
        picked = pltpu.roll(picked, shift, 1)
        kept = picked[0:member_local]
        for q in range(1, members // member_local):
            kept = jnp.where(mine == q, picked[q * member_local : (q + 1) * member_local], kept)
        discharge[hour] = kept[:, 0:basin_local]
        mean = jnp.sum(picked, axis=0, keepdims=True) / members
        ensemble[hour : hour + 1, :] = mean[:, 0:basin_local]


def route_plain(gathered, upstream, reach_level, celerity, storage, mem_local, basin_local):
    reaches = reach_level.shape[0]
    members = gathered.shape[0] * gathered.shape[2] // reaches
    whole = gathered.reshape(members, -1, gathered.shape[1], gathered.shape[2])
    whole = jnp.transpose(whole, (1, 3, 0, 2)).reshape(reaches, members, gathered.shape[1])
    lateral, initial = whole[:, :, :DEC], whole[:, :, DEC]
    speed_rate, store_rate = celerity[:, None], storage[:, None]
    up_index = jnp.where(upstream < 0, reaches, upstream)
    outflow = jnp.zeros_like(lateral)
    for level_now in range(LEVELS):
        padded = jnp.concatenate([outflow, jnp.zeros_like(outflow[:1])], axis=0)
        inflow = padded[up_index[:, 0]]
        for entry in range(1, up_index.shape[1]):
            inflow = inflow + padded[up_index[:, entry]]
        flow = initial
        hours = []
        for hour in range(DEC):
            flow_power = flow**BETA
            target = speed_rate * inflow[:, :, hour] + store_rate * flow_power + lateral[:, :, hour]
            for _ in range(NEWTON):
                flow_power = flow**BETA
                ratio = (target - (1.0 - BETA) * store_rate * flow_power) / (
                    speed_rate * flow + BETA * store_rate * flow_power
                )
                flow = flow * jnp.maximum(ratio, 0.5)
            hours.append(flow)
        routed = jnp.stack(hours, axis=2)
        outflow = jnp.where((reach_level == level_now)[:, None, None], routed, outflow)
    ensemble = jnp.sum(outflow, axis=1) / members
    first_row = lax.axis_index("basin") * basin_local
    mine = lax.dynamic_slice_in_dim(outflow, first_row, basin_local, 0)
    mine = lax.dynamic_slice_in_dim(mine, lax.axis_index("member") * mem_local, mem_local, 1)
    return mine, lax.dynamic_slice_in_dim(ensemble, first_row, basin_local, 0)


def on_device(
    forcing,
    tile_part,
    tile_slot,
    tile_weight,
    w_input,
    w_encoder,
    b_encoder,
    w_decoder,
    b_decoder,
    w_output,
    celerity,
    storage,
    initial_flow,
    reach_level,
    upstream,
):
    tile_local, mem_local, hour_feat = forcing.shape
    part_count = lax.axis_size("basin")
    basin_local = initial_flow.shape[0]
    reaches = reach_level.shape[0]
    groups = part_count // mem_local
    rows = reaches // groups
    width = -(-(hour_feat + 5 * TOP + 3) // LANES) * LANES

    weight_pieces = three_pieces(tile_weight)
    columns = [piece[:, entry] for entry in range(TOP) for piece in weight_pieces]
    columns = columns + [tile_part[:, entry].astype(jnp.float32) for entry in range(TOP)]
    columns = columns + [tile_slot[:, entry].astype(jnp.float32) for entry in range(TOP)]
    extra = jnp.stack(columns, axis=1).astype(jnp.bfloat16)
    extra = jnp.broadcast_to(extra[None], (mem_local,) + extra.shape)
    flow = jnp.stack(three_pieces(initial_flow.T), axis=2).astype(jnp.bfloat16)
    flow = jnp.pad(flow, ((0, 0), (0, tile_local - basin_local), (0, width - hour_feat - 5 * TOP - 3)))
    send = jnp.concatenate([jnp.swapaxes(forcing, 0, 1), extra, flow], axis=2)
    send = jnp.broadcast_to(send[:, None], (mem_local, groups, tile_local, width))
    send = send.reshape(part_count, tile_local, width)
    arrived = lax.all_to_all(send, "basin", split_axis=0, concat_axis=0, tiled=True)

    vmem = pl.BlockSpec(memory_space=pltpu.VMEM)
    sources = min(part_count, 8)
    lateral = pl.pallas_call(
        functools.partial(lstm_kernel, (hour_feat, basin_local, groups, sources)),
        out_shape=jax.ShapeDtypeStruct((8, rows), jnp.float32),
        in_specs=[vmem] * 7,
        out_specs=vmem,
        compiler_params=pltpu.CompilerParams(vmem_limit_bytes=48 << 20),
    )(
        arrived,
        w_input,
        w_encoder,
        b_encoder[None],
        w_decoder,
        b_decoder[None],
        jnp.broadcast_to(w_output[None], (8, w_output.shape[0])),
    )
    axes = ("member", "basin")
    world = lax.axis_size("member") * part_count
    copies = jnp.broadcast_to(lateral[None], (world,) + lateral.shape)
    gathered = lax.all_to_all(copies, axes, split_axis=0, concat_axis=0, tiled=True)
    if reaches > KERNEL_REACHES or rows != LANES:
        return route_plain(gathered, upstream, reach_level, celerity, storage, mem_local, basin_local)
    discharge, ensemble = pl.pallas_call(
        functools.partial(route_kernel, mem_local, basin_local),
        out_shape=(
            jax.ShapeDtypeStruct((DEC, mem_local, basin_local), jnp.float32),
            jax.ShapeDtypeStruct((DEC, basin_local), jnp.float32),
        ),
        in_specs=[vmem] * 5,
        out_specs=(vmem, vmem),
        compiler_params=pltpu.CompilerParams(vmem_limit_bytes=48 << 20),
    )(
        gathered.reshape(world * 8, rows),
        upstream.T,
        reach_level[None],

        celerity[None],
        storage[None],
    )
    return jnp.transpose(discharge, (2, 1, 0)), ensemble.T


def solution(mesh):
    placed = (
        P("basin", "member", None),
        P("basin", None),
        P("basin", None),
        P("basin", None),
        P(),
        P(),
        P(),
        P(),
        P(),
        P(),
        P(),
        P(),
        P("basin", "member"),
        P(),
        P(),
    )
    return jax.shard_map(
        on_device,
        mesh=mesh,
        in_specs=placed,
        out_specs=(P("basin", "member", None), P("basin", None)),
        check_vma=False,
    )
```

time: 179 us -> 43.1 us (0.24)
  blocking collectives: 104 us -> 27.3 us
  local copies, waits for them, and re-layouts: 25.9 us -> 1.82 us
  matrix products: 15.9 us -> 0 us
  starting transfers between devices: 13.3 us -> 0 us
  Pallas kernels: 0 us -> 10.6 us
  waiting for transfers between devices: 8.82 us -> 0 us
  other arithmetic: 8.64 us -> 2.34 us
    all_gather x3 -> x0, blocking collectives: 94 us -> none  [on_device(): gathered = lax.all_gather(outflow, 'basin', axis=0, tiled=True)]
    all_to_all x0 -> x2, blocking collectives: none -> 27.3 us  [the longest x1 16.1 us: on_device(): lax.all_to_all(send, 'basin', split_axis=0, concat_axis=0, tiled=True)]
    dot_general x63 -> x0, matrix products: 15.9 us -> none  [the longest x24 6.59 us: encode(): jnp.dot(forcing_hour, w_input, preferred_element_type=jnp.float32)]
    all_to_all x2 -> x0, starting transfers between devices: 13.3 us -> none  [the longest x1 7.28 us: on_device(): lax.all_to_all(send_slots, 'basin', split_axis=0, concat_axis=0, tiled=True)]
    pallas_call x0 -> x2, Pallas kernels: none -> 10.6 us  [the longest x1 7.78 us: on_device(): pl.pallas_call(functools.partial(lstm_kernel, (hour_feat, basin_local, gr...]
    psum x1 -> x0, blocking collectives: 10.1 us -> none  [on_device(): member_total = lax.psum(jnp.sum(outflow, axis=1), 'member')]
    gather x16 -> x0, local copies, waits for them, and re-layouts: 9.72 us -> none  [the longest x12 7.29 us: route_level(): inflow = inflow + padded[up_index[:, entry]]]
    all_to_all x2 -> x0, waiting for transfers between devices: 8.82 us -> none  [the longest x1 8.81 us: on_device(): lax.all_to_all(send_rows, 'basin', split_axis=0, concat_axis=0, tiled=True)]
  transfers between devices with their start and end apart: 2 -> 0, of which waited for: 1 -> 0; matrix products, arithmetic and copies ran while one was open for 3% -> 0% of each run, Pallas kernels for 0% -> 0%
where the time goes in v1:
time: 43.1 us; the launch traced here: 42.8 us
  blocking collectives  27.3 us (63%)
  Pallas kernels  10.6 us (25%)
  other arithmetic  2.34 us (5%)
  local copies, waits for them, and re-layouts  1.82 us (4%)
  between operations  0.78 us (2%)
    all_to_all x1, blocking collectives, on_device(): lax.all_to_all(send, 'basin', split_axis=0, concat_axis=0, tiled=True)  16.1 us
    all_to_all x1, blocking collectives, on_device(): lax.all_to_all(copies, axes, split_axis=0, concat_axis=0, tiled=True)  11.2 us
    pallas_call x1, Pallas kernels, on_device(): pl.pallas_call(functools.partial(lstm_kernel, (hour_feat, basin_local, gr...  7.78 us
    pallas_call x1, Pallas kernels, on_device(): pl.pallas_call(functools.partial(route_kernel, mem_local, basin_local), o...  2.79 us
    unnamed x23, local copies, waits for them, and re-layouts  1.53 us
    another operation x2, other arithmetic  1.49 us

profile of v1, /device:TPU:0, one launch (start us, length us, event | category | flops | bytes accessed | tf_op | source)
XLA Modules:
  0.0 42.8 jit_solution(291240340386551209)
XLA Ops:
  0.6 0.0 copy-start.9
  0.6 0.7 %fusion.3 = (bf16[64,2]{0,1:T(2,128)(2,1)S(1)}, bf16[64,2]{0,1:T(2,128)(2,1)S(1)}, bf16[64,2]{0,1:T(2,128)(2,1)S(1)}) fusion(f32[64,2]{0,1:T(2,128)} %param.18), kind=kLoop, calls=%fused_computation.13 | loop fusion | flops 896 | bytes 1280 | tf_op jit(solution)/shard_map/convert.19
  1.4 0.8 %convert_convert_fusion = (bf16[64,1]{0,1:T(2,128)(2,1)S(1)}, bf16[64,1]{0,1:T(2,128)(2,1)S(1)}, bf16[64,1]{0,1:T(2,128)(2,1)S(1)}, bf16[64,1]{0,1:T(2,128)(2,1)S(1)}) fusion(s32[64,2]{0,1:T(2,128)} %param.17, s32[64,2]{0,1:T(2,128)} %param.16), kind=kLoop, calls=%fused_computation.17 | loop fusion | flops 512 | bytes 1536 | tf_op jit(solution)/shard_map/convert.15
  2.1 0.1 stack.23
  2.2 0.1 copy.17
  2.3 0.7 %fusion.5 = (bf16[4,32,1]{1,0,2:T(4,128)(2,1)S(1)}, bf16[4,32,1]{1,0,2:T(4,128)(2,1)S(1)}, bf16[4,32,1]{1,0,2:T(4,128)(2,1)S(1)}) fusion(f32[32,4]{0,1:T(4,128)} %param.27), kind=kLoop, calls=%fused_computation.15 | loop fusion | flops 896 | bytes 1280 | tf_op jit(solution)/shard_map/stack | solution.py:249
  3.0 0.1 copy.20
  3.2 0.0 copy-done.9
  3.2 0.2 fusion.1
  3.4 0.0 copy-start.1
  3.4 0.0 copy-start
  3.4 0.0 copy-start.10
  3.4 0.0 copy-start.2
  3.5 16.1 %all_to_all.10.arrived = bf16[8,64,256]{2,1,0:T(8,128)(2,1)S(1)} all-to-all(bf16[8,64,256]{2,1,0:T(8,128)(2,1)S(1)} %bitcast.37), channel_id=1, replica_groups=mesh['basin'=8,'member'=4] {'basin'}, dimensions={0} | all-to-all | bytes 524288 | tf_op jit(solution)/shard_map/all_to_all | solution.py:254
  19.6 0.0 copy-done.10
  19.6 0.0 copy-start.3
  19.6 0.0 copy-start.4
  19.6 0.0 copy-done.1
  19.6 0.0 copy-done
  19.6 0.0 copy-done.2
  19.6 0.6 %copy-done.3 = f32[1024]{0:T(1024)S(1)} copy-done((f32[1024]{0:T(1024)S(1)}, f32[1024]{0:T(1024)}, u32[]{:S(2)}) %copy-start.3) | copy-done | bytes 4120
  20.3 0.0 copy-done.4
  20.3 7.8 %shard_map.158 = f32[8,128]{1,0:T(8,128)S(1)} custom-call(bf16[8,64,256]{2,1,0:T(8,128)(2,1)S(1)} %all_to_all.10.arrived, bf16[8,1024]{1,0:T(8,128)(2,1)S(1)} %copy-done.2, bf16[256,1024]{1,0:T(8,128)(2,1)S(1)} %copy-done, f32[1,1024]{1,0:T(1,128)S(1)} %bitcast.31, bf16[256,1024]{1,0:T(8,128)(2,1)S(1)} %copy-done.1, f32[1,1024]{1,0:T(1,128)S(1)} %bitcast.32, ...), custom_call_target="tpu_custom_call" | custom-call | tf_op jit(solution)/shard_map/pallas_call | solution.py:258
  28.1 0.0 copy-start.7
  28.1 0.0 copy-start.8
  28.2 11.2 %all_to_all.11 = f32[32,8,128]{2,1,0:T(8,128)S(1)} all-to-all(f32[32,8,128]{2,1,0:T(8,128)S(1)} %broadcast_in_dim.44), channel_id=1, replica_groups=mesh['basin'=8,'member'=4] {'member','basin'}, dimensions={0} | all-to-all | bytes 262144 | tf_op jit(solution)/shard_map/all_to_all | solution.py:276
  39.3 0.0 copy-start.5
  39.3 0.0 copy-done.7
  39.3 0.0 copy-done.8
  39.3 0.7 %copy-done.5 = s32[256,4]{0,1:T(4,128)S(1)} copy-done((s32[256,4]{0,1:T(4,128)S(1)}, s32[256,4]{0,1:T(4,128)}, u32[]{:S(2)}) %copy-start.5) | copy-done | bytes 4120
  40.0 0.0 copy-done.6
  40.0 2.8 %shard_map.159 = (f32[6,4,32]{2,1,0:T(4,128)}, f32[6,32]{1,0:T(8,128)}) custom-call(f32[256,128]{1,0:T(8,128)S(1)} %bitcast.30, s32[4,256]{1,0:T(4,128)S(1)} %bitcast.33, s32[1,256]{1,0:T(1,128)S(1)} %bitcast.34, f32[1,256]{1,0:T(1,128)S(1)} %bitcast.35, f32[1,256]{1,0:T(1,128)S(1)} %bitcast.36), custom_call_target="tpu_custom_call" | custom-call | tf_op jit(solution)/shard_map/pallas_call | solution.py:279
  (9 shorter events, 0.1 us)
Async XLA Ops:
  0.6 2.6 %copy-start.9 = (bf16[64,4,192]{2,1,0:T(4,128)(2,1)S(1)}, bf16[64,4,192]{2,1,0:T(4,128)(2,1)}, u32[]{:S(2)}) copy-start(bf16[64,4,192]{2,1,0:T(4,128)(2,1)} %param.15) | copy-start | bytes 294916
  3.4 16.2 %copy-start.1 = (bf16[256,1024]{1,0:T(8,128)(2,1)S(1)}, bf16[256,1024]{1,0:T(8,128)(2,1)}, u32[]{:S(2)}) copy-start(bf16[256,1024]{1,0:T(8,128)(2,1)} %w_decoder.1) | copy-start | bytes 1572868
  3.4 16.2 %copy-start = (bf16[256,1024]{1,0:T(8,128)(2,1)S(1)}, bf16[256,1024]{1,0:T(8,128)(2,1)}, u32[]{:S(2)}) copy-start(bf16[256,1024]{1,0:T(8,128)(2,1)} %w_encoder.1) | copy-start | bytes 1572868
  3.4 16.2 %copy-start.10 = (bf16[256]{0:T(256)(128)(2,1)S(1)}, bf16[256]{0:T(256)(128)(2,1)}, u32[]{:S(2)}) copy-start(bf16[256]{0:T(256)(128)(2,1)} %param.24) | copy-start | bytes 1540
  3.4 16.2 %copy-start.2 = (bf16[8,1024]{1,0:T(8,128)(2,1)S(1)}, bf16[8,1024]{1,0:T(8,128)(2,1)}, u32[]{:S(2)}) copy-start(bf16[8,1024]{1,0:T(8,128)(2,1)} %w_input.1) | copy-start | bytes 49156
  19.6 0.7 %copy-start.3 = (f32[1024]{0:T(1024)S(1)}, f32[1024]{0:T(1024)}, u32[]{:S(2)}) copy-start(f32[1024]{0:T(1024)} %param.21) | copy-start | bytes 12292
  19.6 0.7 %copy-start.4 = (f32[1024]{0:T(1024)S(1)}, f32[1024]{0:T(1024)}, u32[]{:S(2)}) copy-start(f32[1024]{0:T(1024)} %param.23) | copy-start | bytes 12292
  28.1 11.2 %copy-start.7 = (f32[256]{0:T(256)S(1)}, f32[256]{0:T(256)}, u32[]{:S(2)}) copy-start(f32[256]{0:T(256)} %param.25) | copy-start | bytes 3076
  28.1 11.2 %copy-start.8 = (f32[256]{0:T(256)S(1)}, f32[256]{0:T(256)}, u32[]{:S(2)}) copy-start(f32[256]{0:T(256)} %param.26) | copy-start | bytes 3076
  39.3 0.7 %copy-start.5 = (s32[256,4]{0,1:T(4,128)S(1)}, s32[256,4]{0,1:T(4,128)}, u32[]{:S(2)}) copy-start(s32[256,4]{0,1:T(4,128)} %param.29) | copy-start | bytes 12292
  39.3 0.7 %copy-start.6 = (s32[256]{0:T(256)S(1)}, s32[256]{0:T(256)}, u32[]{:S(2)}) copy-start(s32[256]{0:T(256)} %param.28) | copy-start | bytes 3076

commit v2 on v1

--- a/solution.py
+++ b/solution.py
@@ -15,15 +15,9 @@
 BETA = 0.6
 LANES = 128
 KERNEL_REACHES = 512
+EXTRAS = 16
 
 dot = functools.partial(jnp.dot, preferred_element_type=jnp.float32)
-
-
-def three_pieces(values):
-    high = lax.reduce_precision(values, 8, 7)
-    rest = values - high
-    middle = lax.reduce_precision(rest, 8, 7)
-    return [high, middle, rest - middle]
 
 
 def cell_update(gate_sum, memory_cell):
@@ -37,38 +31,82 @@
     return hidden, memory_cell
 
 
+def pack_kernel(
+    forcing, part, slot, weight, flow, b_encoder, b_decoder, tables, send, small
+):
+    members, tile_local, width = forcing.shape
+    groups = send.shape[0] // members
+    basin_local = flow.shape[1]
+    half = tile_local // 2
+
+    def pieces(values):
+        high = values.astype(jnp.bfloat16).astype(jnp.float32)
+        rest = values - high
+        middle = rest.astype(jnp.bfloat16).astype(jnp.float32)
+        return [high, middle, rest - middle]
+
+    def side_by_side(rows):
+        return jnp.concatenate([rows[entry : entry + 1] for entry in range(TOP)], axis=1)
+
+    common = pieces(side_by_side(weight[...]))
+    common += [side_by_side(part[...].astype(jnp.float32)), side_by_side(slot[...].astype(jnp.float32))]
+    owners = LANES // basin_local
+    lane = lax.broadcasted_iota(jnp.int32, (1, LANES), 1)
+    mine = lane // basin_local == lax.rem(lax.axis_index("basin"), owners)
+    for member in range(members):
+        tiles = forcing[member]
+        first = tiles[:, :LANES]
+        second = jnp.concatenate([tiles[:half, LANES:], tiles[half:, LANES:]], axis=1)
+        own_flow = jnp.concatenate([flow[member : member + 1, :]] * owners, axis=1)
+        rows = common + pieces(jnp.where(mine, own_flow, 0.0))
+        rows.append(jnp.zeros((EXTRAS - len(rows), LANES), jnp.float32))
+        extras = jnp.concatenate(rows, axis=0).astype(jnp.bfloat16)
+        for group in range(groups):
+            device = member * groups + group
+            send[device, :tile_local, :] = first
+            send[device, tile_local : tile_local + half, :] = second
+            send[device, tile_local + half :, :] = extras
+    small[0:1, : b_encoder.shape[1]] = b_encoder[...]
+    small[1:2, : b_decoder.shape[1]] = b_decoder[...]
+    at = 2
+    for table in tables:
+        count, length = table.shape
+        small[at : at + count, :length] = table[...].astype(jnp.float32)
+        at += count
+
+
 def lstm_kernel(
-    shape, arrived, w_input, w_encoder, b_encoder, w_decoder, b_decoder, w_output, out
+    shape, arrived, w_input, w_encoder, w_decoder, w_output, small, out
 ):
-    hour_feat, basin_local, groups, sources = shape
+    hour_feat, tile_local, basin_local, groups, sources = shape
     hours = hour_feat // FEAT
-    devices, tile_local, _ = arrived.shape
+    devices = arrived.shape[0]
     rows = out.shape[1]
     units = w_encoder.shape[0]
     half = lax.rem(lax.axis_index("basin"), groups)
-    first = half * rows
-    extra_at = hour_feat // LANES * LANES
-    lane0 = hour_feat - extra_at
+    first = (half * rows).astype(jnp.float32)
+    folded = tile_local // 2
+    extra_at = tile_local + folded
 
     def add_sources(chunk, total):
-        block = arrived[pl.ds(chunk * sources, sources)]
-        block = block.reshape(sources * tile_local, block.shape[2]).astype(jnp.float32)
-        extra = block[:, extra_at : extra_at + LANES]
-        across = extra.T
-        for entry in range(TOP):
-            col = lane0 + 3 * entry
-            weight = extra[:, col : col + 1] + extra[:, col + 1 : col + 2] + extra[:, col + 2 : col + 3]
-            term = (weight * block).astype(jnp.bfloat16)
-            part = lane0 + 3 * TOP + entry
-            slot = part + TOP
-            basin = across[part : part + 1] * basin_local + across[slot : slot + 1]
-            basin = basin.astype(jnp.int32) - first
-            row_of = lax.broadcasted_iota(jnp.int32, (rows, sources * tile_local), 0)
-            picked = jnp.where(row_of == basin, 1.0, 0.0).astype(jnp.bfloat16)
-            total = total + dot(picked, term)
-        return total
-
-    total = jnp.zeros((rows, arrived.shape[2]), jnp.float32)
+        block = arrived[pl.ds(chunk * sources, sources)].astype(jnp.float32)
+        extras = block[:, extra_at:, :]
+        weight = extras[:, 0] + extras[:, 1] + extras[:, 2]
+        basin = extras[:, 3] * basin_local + extras[:, 4] - first
+        weight = weight.T
+        row_of = lax.broadcasted_iota(jnp.int32, (rows, TOP * tile_local), 0).astype(jnp.float32)
+        picked, terms = [], []
+        for source in range(sources):
+            picked.append(jnp.where(row_of == basin[source : source + 1], 1.0, 0.0).astype(jnp.bfloat16))
+            second = block[source, tile_local:extra_at, :]
+            second = jnp.concatenate([second, pltpu.roll(second, LANES // 2, 1)], axis=0)
+            tiles = jnp.concatenate([block[source, :tile_local, :], second], axis=1)
+            for entry in range(TOP):
+                column = weight[entry * tile_local : (entry + 1) * tile_local, source : source + 1]
+                terms.append((column * tiles).astype(jnp.bfloat16))
+        return total + dot(jnp.concatenate(picked, axis=1), jnp.concatenate(terms, axis=0))
+
+    total = jnp.zeros((rows, 2 * LANES), jnp.float32)
     if devices == sources:
         total = add_sources(0, total)
     else:
@@ -76,21 +114,20 @@
     inputs = total.astype(jnp.bfloat16)
 
     owners = rows // basin_local
-    flow = arrived[pl.ds(half * owners, owners), 0:basin_local, extra_at : extra_at + LANES]
-    flow = flow.astype(jnp.float32).reshape(rows, LANES).T
-    at = lane0 + 5 * TOP
-    flow = flow[at : at + 1] + flow[at + 1 : at + 2] + flow[at + 2 : at + 3]
-    out[DEC : DEC + 1, :] = flow
+    flow = arrived[pl.ds(half * owners, owners), extra_at:, :].astype(jnp.float32)
+    flow = jnp.sum(flow, axis=0)
+    out[DEC : DEC + 1, :] = flow[5:6] + flow[6:7] + flow[7:8]
     out[DEC + 1 :, :] = jnp.zeros((out.shape[0] - DEC - 1, rows), jnp.float32)
+    b_encoder, b_decoder = small[0:1, : 4 * units], small[1:2, : 4 * units]
 
     hidden = jnp.zeros((rows, units), jnp.bfloat16)
     memory_cell = jnp.zeros((rows, units), jnp.float32)
     for hour in range(hours):
-        gate_sum = dot(inputs[:, hour * FEAT : (hour + 1) * FEAT], w_input[...]) + b_encoder[...]
+        gate_sum = dot(inputs[:, hour * FEAT : (hour + 1) * FEAT], w_input[...]) + b_encoder
         gate_sum = gate_sum + dot(hidden, w_encoder[...])
         hidden, memory_cell = cell_update(gate_sum, memory_cell)
     for hour in range(DEC):
-        gate_sum = dot(hidden, w_decoder[...]) + b_decoder[...]
+        gate_sum = dot(hidden, w_decoder[...]) + b_decoder
         hidden, memory_cell = cell_update(gate_sum, memory_cell)
         runoff = lax.dot_general(
             w_output[...], hidden, (((1,), (1,)), ((), ())), preferred_element_type=jnp.float32
@@ -103,19 +140,20 @@
     return jnp.exp(BETA * jnp.log(flow))
 
 
-def route_kernel(member_local, basin_local, gathered, upstream, level_row, celerity, storage, discharge, ensemble):
-    reaches = level_row.shape[1]
+def route_kernel(member_local, basin_local, reaches, gathered, small, discharge, ensemble):
+    celerity, storage, level_row = small[2:3, :reaches], small[3:4, :reaches], small[4:5, :reaches]
+    upstream = small[5:9, :reaches]
     halves = reaches // LANES
     per_member = halves * 8
     members = gathered.shape[0] // per_member
-    levels = jnp.broadcast_to(level_row[...], (members, reaches))
-    source = lax.broadcasted_iota(jnp.int32, (reaches, reaches), 0)
+    levels = jnp.broadcast_to(level_row, (members, reaches)).astype(jnp.int32)
+    source = lax.broadcasted_iota(jnp.int32, (reaches, reaches), 0).astype(jnp.float32)
     links = jnp.zeros((reaches, reaches), jnp.float32)
     for entry in range(upstream.shape[0]):
         links = links + jnp.where(source == upstream[entry : entry + 1, :], 1.0, 0.0)
     links = links.astype(jnp.bfloat16)
-    speed_rate = jnp.broadcast_to(celerity[...], (members, reaches))
-    store_rate = jnp.broadcast_to(storage[...], (members, reaches))
+    speed_rate = jnp.broadcast_to(celerity, (members, reaches))
+    store_rate = jnp.broadcast_to(storage, (members, reaches))
 
     def row(k):
         return jnp.concatenate(
@@ -238,61 +276,62 @@
     reaches = reach_level.shape[0]
     groups = part_count // mem_local
     rows = reaches // groups
-    width = -(-(hour_feat + 5 * TOP + 3) // LANES) * LANES
-
-    weight_pieces = three_pieces(tile_weight)
-    columns = [piece[:, entry] for entry in range(TOP) for piece in weight_pieces]
-    columns = columns + [tile_part[:, entry].astype(jnp.float32) for entry in range(TOP)]
-    columns = columns + [tile_slot[:, entry].astype(jnp.float32) for entry in range(TOP)]
-    extra = jnp.stack(columns, axis=1).astype(jnp.bfloat16)
-    extra = jnp.broadcast_to(extra[None], (mem_local,) + extra.shape)
-    flow = jnp.stack(three_pieces(initial_flow.T), axis=2).astype(jnp.bfloat16)
-    flow = jnp.pad(flow, ((0, 0), (0, tile_local - basin_local), (0, width - hour_feat - 5 * TOP - 3)))
-    send = jnp.concatenate([jnp.swapaxes(forcing, 0, 1), extra, flow], axis=2)
-    send = jnp.broadcast_to(send[:, None], (mem_local, groups, tile_local, width))
-    send = send.reshape(part_count, tile_local, width)
+    in_kernel = reaches <= KERNEL_REACHES and rows == LANES
+    tables = (celerity[None], storage[None], reach_level[None], upstream.T) if in_kernel else ()
+
+    vmem = pl.BlockSpec(memory_space=pltpu.VMEM)
+    params = pltpu.CompilerParams(vmem_limit_bytes=48 << 20)
+    send, small = pl.pallas_call(
+        pack_kernel,
+        out_shape=(
+            jax.ShapeDtypeStruct((part_count, tile_local + tile_local // 2 + EXTRAS, LANES), jnp.bfloat16),
+            jax.ShapeDtypeStruct((16, b_encoder.shape[0]), jnp.float32),
+        ),
+        in_specs=[vmem] * 7 + [(vmem,) * len(tables)],
+        out_specs=(vmem, vmem),
+        compiler_params=params,
+    )(
+        jnp.swapaxes(forcing, 0, 1),
+        tile_part.T,
+        tile_slot.T,
+        tile_weight.T,
+        initial_flow.T,
+        b_encoder[None],
+        b_decoder[None],
+        tables,
+    )
     arrived = lax.all_to_all(send, "basin", split_axis=0, concat_axis=0, tiled=True)
-
-    vmem = pl.BlockSpec(memory_space=pltpu.VMEM)
     sources = min(part_count, 8)
     lateral = pl.pallas_call(
-        functools.partial(lstm_kernel, (hour_feat, basin_local, groups, sources)),
+        functools.partial(lstm_kernel, (hour_feat, tile_local, basin_local, groups, sources)),
         out_shape=jax.ShapeDtypeStruct((8, rows), jnp.float32),
-        in_specs=[vmem] * 7,
+        in_specs=[vmem] * 6,
         out_specs=vmem,
-        compiler_params=pltpu.CompilerParams(vmem_limit_bytes=48 << 20),
+        compiler_params=params,
     )(
         arrived,
         w_input,
         w_encoder,
-        b_encoder[None],
         w_decoder,
-        b_decoder[None],
         jnp.broadcast_to(w_output[None], (8, w_output.shape[0])),
+        small,
     )
     axes = ("member", "basin")
     world = lax.axis_size("member") * part_count
     copies = jnp.broadcast_to(lateral[None], (world,) + lateral.shape)
     gathered = lax.all_to_all(copies, axes, split_axis=0, concat_axis=0, tiled=True)
-    if reaches > KERNEL_REACHES or rows != LANES:
+    if not in_kernel:
         return route_plain(gathered, upstream, reach_level, celerity, storage, mem_local, basin_local)
     discharge, ensemble = pl.pallas_call(
-        functools.partial(route_kernel, mem_local, basin_local),
+        functools.partial(route_kernel, mem_local, basin_local, reaches),
         out_shape=(
             jax.ShapeDtypeStruct((DEC, mem_local, basin_local), jnp.float32),
             jax.ShapeDtypeStruct((DEC, basin_local), jnp.float32),
         ),
-        in_specs=[vmem] * 5,
+        in_specs=[vmem] * 2,
         out_specs=(vmem, vmem),
-        compiler_params=pltpu.CompilerParams(vmem_limit_bytes=48 << 20),
-    )(
-        gathered.reshape(world * 8, rows),
-        upstream.T,
-        reach_level[None],
-
-        celerity[None],
-        storage[None],
-    )
+        compiler_params=params,
+    )(gathered.reshape(world * 8, rows), small)
     return jnp.transpose(discharge, (2, 1, 0)), ensemble.T
 
 

time: 43.1 us -> 47.8 us (1.11)
  local copies, waits for them, and re-layouts: 1.82 us -> 9.52 us
  other arithmetic: 2.34 us -> 0 us
  blocking collectives: 27.3 us -> 26.4 us
    unnamed x23 -> x29, local copies, waits for them, and re-layouts: 1.53 us -> 9.49 us
    another operation x4 -> x0, other arithmetic: 2.19 us -> none
    all_to_all x1, blocking collectives: 16.1 us -> 15.5 us  [on_device(): lax.all_to_all(send, 'basin', split_axis=0, concat_axis=0, tiled=True)]
    pallas_call x2 -> x3, Pallas kernels: 10.6 us -> 10.6 us  [the longest x1 7.74 us: on_device(): pl.pallas_call(functools.partial(lstm_kernel, (hour_feat, tile_local, bas...]
where the time goes in v2:
time: 47.8 us; the launch traced here: 47.3 us
  blocking collectives  26.4 us (55%)
  Pallas kernels  10.6 us (22%)
  local copies, waits for them, and re-layouts  9.52 us (20%)
  between operations  0.69 us (1%)
    all_to_all x1, blocking collectives, on_device(): lax.all_to_all(send, 'basin', split_axis=0, concat_axis=0, tiled=True)  15.5 us
    all_to_all x1, blocking collectives, on_device(): lax.all_to_all(copies, axes, split_axis=0, concat_axis=0, tiled=True)  10.9 us
    unnamed x29, local copies, waits for them, and re-layouts  9.49 us
    pallas_call x1, Pallas kernels, on_device(): pl.pallas_call(functools.partial(lstm_kernel, (hour_feat, tile_local, bas...  7.74 us
    pallas_call x1, Pallas kernels, on_device(): pl.pallas_call(functools.partial(route_kernel, mem_local, basin_local, re...  2.79 us

profile of v2, /device:TPU:0, one launch (start us, length us, event | category | flops | bytes accessed | tf_op | source)
XLA Modules:
  0.0 47.3 jit_solution(9287095450025067936)
XLA Ops:
  0.6 0.0 copy-start
  0.6 1.0 %copy.19 = bf16[64,4,192]{2,0,1:T(8,128)(2,1)S(1)} copy(bf16[64,4,192]{2,1,0:T(4,128)(2,1)} %param.15) | data formatting | bytes 196608 | tf_op args[0]
  1.6 0.0 copy-start.3
  1.6 0.7 %copy-done.3 = f32[1024]{0:T(1024)S(1)} copy-done((f32[1024]{0:T(1024)S(1)}, f32[1024]{0:T(1024)}, u32[]{:S(2)}) %copy-start.3) | copy-done | bytes 4120
  2.3 0.0 copy-start.4
  2.3 0.7 %copy-done.4 = f32[1024]{0:T(1024)S(1)} copy-done((f32[1024]{0:T(1024)S(1)}, f32[1024]{0:T(1024)}, u32[]{:S(2)}) %copy-start.4) | copy-done | bytes 4120
  3.0 0.0 copy-start.5
  3.0 0.7 %copy-done.5 = s32[256,4]{0,1:T(4,128)S(1)} copy-done((s32[256,4]{0,1:T(4,128)S(1)}, s32[256,4]{0,1:T(4,128)}, u32[]{:S(2)}) %copy-start.5) | copy-done | bytes 4120
  3.7 0.7 %copy-done.6 = f32[32,4]{0,1:T(4,128)S(1)} copy-done((f32[32,4]{0,1:T(4,128)S(1)}, f32[32,4]{0,1:T(4,128)}, u32[]{:S(2)}) %copy-start.6) | copy-done | bytes 536
  4.4 0.0 copy-start.7
  4.4 0.7 %copy-done.7 = s32[64,2]{0,1:T(2,128)S(1)} copy-done((s32[64,2]{0,1:T(2,128)S(1)}, s32[64,2]{0,1:T(2,128)}, u32[]{:S(2)}) %copy-start.7) | copy-done | bytes 536
  5.0 0.0 copy-start.8
  5.0 0.7 %copy-done.8 = s32[64,2]{0,1:T(2,128)S(1)} copy-done((s32[64,2]{0,1:T(2,128)S(1)}, s32[64,2]{0,1:T(2,128)}, u32[]{:S(2)}) %copy-start.8) | copy-done | bytes 536
  5.7 0.0 copy-start.9
  5.7 0.7 %copy-done.9 = f32[64,2]{0,1:T(2,128)S(1)} copy-done((f32[64,2]{0,1:T(2,128)S(1)}, f32[64,2]{0,1:T(2,128)}, u32[]{:S(2)}) %copy-start.9) | copy-done | bytes 536
  6.4 0.0 copy-start.10
  6.4 0.7 %copy-done.10 = f32[256]{0:T(256)S(1)} copy-done((f32[256]{0:T(256)S(1)}, f32[256]{0:T(256)}, u32[]{:S(2)}) %copy-start.10) | copy-done | bytes 1048
  7.1 0.7 %copy-done.11 = f32[256]{0:T(256)S(1)} copy-done((f32[256]{0:T(256)S(1)}, f32[256]{0:T(256)}, u32[]{:S(2)}) %copy-start.11) | copy-done | bytes 1048
  7.8 0.0 copy-start.12
  7.8 0.7 %copy-done.12 = s32[256]{0:T(256)S(1)} copy-done((s32[256]{0:T(256)S(1)}, s32[256]{0:T(256)}, u32[]{:S(2)}) %copy-start.12) | copy-done | bytes 1048
  8.4 0.1 shard_map.158
  8.5 0.0 copy-start.2
  8.6 15.5 %all_to_all.10.arrived = bf16[8,112,128]{2,1,0:T(8,128)(2,1)S(1)} all-to-all(bf16[8,112,128]{2,1,0:T(8,128)(2,1)S(1)} %get-tuple-element.6), channel_id=1, replica_groups=mesh['basin'=8,'member'=4] {'basin'}, dimensions={0} | all-to-all | bytes 458752 | tf_op jit(solution)/shard_map/all_to_all | solution.py:303
  24.1 0.0 copy-start.13
  24.1 0.7 %copy-done.13 = bf16[256]{0:T(256)(128)(2,1)S(1)} copy-done((bf16[256]{0:T(256)(128)(2,1)S(1)}, bf16[256]{0:T(256)(128)(2,1)}, u32[]{:S(2)}) %copy-start.13) | copy-done | bytes 536
  24.7 0.0 copy-done
  24.7 0.0 copy-done.2
  24.7 0.0 copy-start.1
  24.8 1.0 %copy-done.1 = bf16[256,1024]{1,0:T(8,128)(2,1)S(1)} copy-done((bf16[256,1024]{1,0:T(8,128)(2,1)S(1)}, bf16[256,1024]{1,0:T(8,128)(2,1)}, u32[]{:S(2)}) %copy-start.1) | copy-done | bytes 524312
  25.8 7.7 %shard_map.159 = f32[8,128]{1,0:T(8,128)S(1)} custom-call(bf16[8,112,128]{2,1,0:T(8,128)(2,1)S(1)} %all_to_all.10.arrived, bf16[8,1024]{1,0:T(8,128)(2,1)S(1)} %copy-done.2, bf16[256,1024]{1,0:T(8,128)(2,1)S(1)} %copy-done, bf16[256,1024]{1,0:T(8,128)(2,1)S(1)} %copy-done.1, bf16[8,256]{1,0:T(8,128)(2,1)S(1)} %broadcast_in_dim.32.w_output, ...), custom_call_target="tpu_custom_call" | custom-call | tf_op jit(solution)/shard_map/pallas_call | solution.py:305
  33.6 10.9 %all_to_all.11 = f32[32,8,128]{2,1,0:T(8,128)S(1)} all-to-all(f32[32,8,128]{2,1,0:T(8,128)S(1)} %broadcast_in_dim.33), channel_id=1, replica_groups=mesh['basin'=8,'member'=4] {'member','basin'}, dimensions={0} | all-to-all | bytes 262144 | tf_op jit(solution)/shard_map/all_to_all | solution.py:322
  44.5 2.8 %shard_map.160 = (f32[6,4,32]{2,1,0:T(4,128)}, f32[6,32]{1,0:T(8,128)}) custom-call(f32[256,128]{1,0:T(8,128)S(1)} %bitcast.16, f32[16,1024]{1,0:T(8,128)S(1)} %get-tuple-element.7.small), custom_call_target="tpu_custom_call" | custom-call | tf_op jit(solution)/shard_map/pallas_call | solution.py:325
  (4 shorter events, 0.0 us)
Async XLA Ops:
  0.6 24.1 %copy-start = (bf16[256,1024]{1,0:T(8,128)(2,1)S(1)}, bf16[256,1024]{1,0:T(8,128)(2,1)}, u32[]{:S(2)}) copy-start(bf16[256,1024]{1,0:T(8,128)(2,1)} %w_encoder.1) | copy-start | bytes 1572868
  1.6 0.7 %copy-start.3 = (f32[1024]{0:T(1024)S(1)}, f32[1024]{0:T(1024)}, u32[]{:S(2)}) copy-start(f32[1024]{0:T(1024)} %param.21) | copy-start | bytes 12292
  2.3 0.7 %copy-start.4 = (f32[1024]{0:T(1024)S(1)}, f32[1024]{0:T(1024)}, u32[]{:S(2)}) copy-start(f32[1024]{0:T(1024)} %param.23) | copy-start | bytes 12292
  3.0 0.7 %copy-start.5 = (s32[256,4]{0,1:T(4,128)S(1)}, s32[256,4]{0,1:T(4,128)}, u32[]{:S(2)}) copy-start(s32[256,4]{0,1:T(4,128)} %param.29) | copy-start | bytes 12292
  3.7 0.7 %copy-start.6 = (f32[32,4]{0,1:T(4,128)S(1)}, f32[32,4]{0,1:T(4,128)}, u32[]{:S(2)}) copy-start(f32[32,4]{0,1:T(4,128)} %param.27) | copy-start | bytes 1540
  4.4 0.7 %copy-start.7 = (s32[64,2]{0,1:T(2,128)S(1)}, s32[64,2]{0,1:T(2,128)}, u32[]{:S(2)}) copy-start(s32[64,2]{0,1:T(2,128)} %param.16) | copy-start | bytes 1540
  5.0 0.7 %copy-start.8 = (s32[64,2]{0,1:T(2,128)S(1)}, s32[64,2]{0,1:T(2,128)}, u32[]{:S(2)}) copy-start(s32[64,2]{0,1:T(2,128)} %param.17) | copy-start | bytes 1540
  5.7 0.7 %copy-start.9 = (f32[64,2]{0,1:T(2,128)S(1)}, f32[64,2]{0,1:T(2,128)}, u32[]{:S(2)}) copy-start(f32[64,2]{0,1:T(2,128)} %param.18) | copy-start | bytes 1540
  6.4 0.7 %copy-start.10 = (f32[256]{0:T(256)S(1)}, f32[256]{0:T(256)}, u32[]{:S(2)}) copy-start(f32[256]{0:T(256)} %param.25) | copy-start | bytes 3076
  7.1 0.7 %copy-start.11 = (f32[256]{0:T(256)S(1)}, f32[256]{0:T(256)}, u32[]{:S(2)}) copy-start(f32[256]{0:T(256)} %param.26) | copy-start | bytes 3076
  7.8 0.7 %copy-start.12 = (s32[256]{0:T(256)S(1)}, s32[256]{0:T(256)}, u32[]{:S(2)}) copy-start(s32[256]{0:T(256)} %param.28) | copy-start | bytes 3076
  8.5 16.2 %copy-start.2 = (bf16[8,1024]{1,0:T(8,128)(2,1)S(1)}, bf16[8,1024]{1,0:T(8,128)(2,1)}, u32[]{:S(2)}) copy-start(bf16[8,1024]{1,0:T(8,128)(2,1)} %w_input.1) | copy-start | bytes 49156
  24.1 0.7 %copy-start.13 = (bf16[256]{0:T(256)(128)(2,1)S(1)}, bf16[256]{0:T(256)(128)(2,1)}, u32[]{:S(2)}) copy-start(bf16[256]{0:T(256)(128)(2,1)} %param.24) | copy-start | bytes 1540
  24.7 1.0 %copy-start.1 = (bf16[256,1024]{1,0:T(8,128)(2,1)S(1)}, bf16[256,1024]{1,0:T(8,128)(2,1)}, u32[]{:S(2)}) copy-start(bf16[256,1024]{1,0:T(8,128)(2,1)} %w_decoder.1) | copy-start | bytes 1572868

commit v3 on v2

--- a/solution.py
+++ b/solution.py
@@ -16,27 +16,48 @@
 LANES = 128
 KERNEL_REACHES = 512
 EXTRAS = 16
+INPUT_ROW = 16
 
 dot = functools.partial(jnp.dot, preferred_element_type=jnp.float32)
 
 
 def cell_update(gate_sum, memory_cell):
     units = memory_cell.shape[-1]
-    input_gate = 0.5 * jnp.tanh(0.5 * gate_sum[:, :units]) + 0.5
-    forget_gate = 0.5 * jnp.tanh(0.5 * gate_sum[:, units : 2 * units]) + 0.5
+    input_gate = 0.5 * jnp.tanh(gate_sum[:, :units]) + 0.5
+    forget_gate = 0.5 * jnp.tanh(gate_sum[:, units : 2 * units]) + 0.5
     candidate = jnp.tanh(gate_sum[:, 2 * units : 3 * units])
-    output_gate = 0.5 * jnp.tanh(0.5 * gate_sum[:, 3 * units :]) + 0.5
+    output_gate = 0.5 * jnp.tanh(gate_sum[:, 3 * units :]) + 0.5
     memory_cell = forget_gate * memory_cell + input_gate * candidate
     hidden = (output_gate * jnp.tanh(memory_cell)).astype(jnp.bfloat16)
     return hidden, memory_cell
 
 
-def pack_kernel(
-    forcing, part, slot, weight, flow, b_encoder, b_decoder, tables, send, small
-):
-    members, tile_local, width = forcing.shape
+def stacked(height, width, parts):
+    total = jnp.zeros((height, width), jnp.float32)
+    at = 0
+    for rows in parts:
+        count, length = rows.shape
+        total = total + jnp.pad(
+            rows.astype(jnp.float32), ((at, height - at - count), (0, width - length))
+        )
+        at += count
+    return total
+
+
+def pack_kernel(basin_local, *refs):
+    count = len(refs) // 2 - 1
+    sources, send, held, semaphores = refs[:count], refs[count], refs[count + 1 : -1], refs[-1]
+    copies = [
+        pltpu.make_async_copy(source, target, semaphores.at[i])
+        for i, (source, target) in enumerate(zip(sources, held, strict=True))
+    ]
+    for copy in copies:
+        copy.start()
+    for copy in copies:
+        copy.wait()
+    forcing, weight, part, slot, flow = held
+    tile_local, members, width = forcing.shape
     groups = send.shape[0] // members
-    basin_local = flow.shape[1]
     half = tile_local // 2
 
     def pieces(values):
@@ -54,10 +75,11 @@
     lane = lax.broadcasted_iota(jnp.int32, (1, LANES), 1)
     mine = lane // basin_local == lax.rem(lax.axis_index("basin"), owners)
     for member in range(members):
-        tiles = forcing[member]
+        tiles = forcing[:, member, :]
         first = tiles[:, :LANES]
         second = jnp.concatenate([tiles[:half, LANES:], tiles[half:, LANES:]], axis=1)
-        own_flow = jnp.concatenate([flow[member : member + 1, :]] * owners, axis=1)
+        own_flow = flow[member : member + 1, :]
+        own_flow = jnp.concatenate([own_flow] * owners, axis=1)
         rows = common + pieces(jnp.where(mine, own_flow, 0.0))
         rows.append(jnp.zeros((EXTRAS - len(rows), LANES), jnp.float32))
         extras = jnp.concatenate(rows, axis=0).astype(jnp.bfloat16)
@@ -66,17 +88,10 @@
             send[device, :tile_local, :] = first
             send[device, tile_local : tile_local + half, :] = second
             send[device, tile_local + half :, :] = extras
-    small[0:1, : b_encoder.shape[1]] = b_encoder[...]
-    small[1:2, : b_decoder.shape[1]] = b_decoder[...]
-    at = 2
-    for table in tables:
-        count, length = table.shape
-        small[at : at + count, :length] = table[...].astype(jnp.float32)
-        at += count
 
 
 def lstm_kernel(
-    shape, arrived, w_input, w_encoder, w_decoder, w_output, small, out
+    shape, arrived, small, w_encoder, w_decoder, out
 ):
     hour_feat, tile_local, basin_local, groups, sources = shape
     hours = hour_feat // FEAT
@@ -119,18 +134,20 @@
     out[DEC : DEC + 1, :] = flow[5:6] + flow[6:7] + flow[7:8]
     out[DEC + 1 :, :] = jnp.zeros((out.shape[0] - DEC - 1, rows), jnp.float32)
     b_encoder, b_decoder = small[0:1, : 4 * units], small[1:2, : 4 * units]
+    w_input = small[INPUT_ROW : INPUT_ROW + FEAT, : 4 * units].astype(jnp.bfloat16)
+    w_output = jnp.broadcast_to(small[2:3, :units], (8, units)).astype(jnp.bfloat16)
 
     hidden = jnp.zeros((rows, units), jnp.bfloat16)
     memory_cell = jnp.zeros((rows, units), jnp.float32)
     for hour in range(hours):
-        gate_sum = dot(inputs[:, hour * FEAT : (hour + 1) * FEAT], w_input[...]) + b_encoder
+        gate_sum = dot(inputs[:, hour * FEAT : (hour + 1) * FEAT], w_input) + b_encoder
         gate_sum = gate_sum + dot(hidden, w_encoder[...])
         hidden, memory_cell = cell_update(gate_sum, memory_cell)
     for hour in range(DEC):
         gate_sum = dot(hidden, w_decoder[...]) + b_decoder
         hidden, memory_cell = cell_update(gate_sum, memory_cell)
         runoff = lax.dot_general(
-            w_output[...], hidden, (((1,), (1,)), ((), ())), preferred_element_type=jnp.float32
+            w_output, hidden, (((1,), (1,)), ((), ())), preferred_element_type=jnp.float32
         )[0:1]
         runoff = jnp.maximum(runoff, 0.0) + jnp.log(1.0 + jnp.exp(-jnp.abs(runoff)))
         out[hour : hour + 1, :] = runoff
@@ -141,8 +158,8 @@
 
 
 def route_kernel(member_local, basin_local, reaches, gathered, small, discharge, ensemble):
-    celerity, storage, level_row = small[2:3, :reaches], small[3:4, :reaches], small[4:5, :reaches]
-    upstream = small[5:9, :reaches]
+    celerity, storage, level_row = small[3:4, :reaches], small[4:5, :reaches], small[5:6, :reaches]
+    upstream = small[6:10, :reaches]
     halves = reaches // LANES
     per_member = halves * 8
     members = gathered.shape[0] // per_member
@@ -281,41 +298,34 @@
 
     vmem = pl.BlockSpec(memory_space=pltpu.VMEM)
     params = pltpu.CompilerParams(vmem_limit_bytes=48 << 20)
-    send, small = pl.pallas_call(
-        pack_kernel,
-        out_shape=(
-            jax.ShapeDtypeStruct((part_count, tile_local + tile_local // 2 + EXTRAS, LANES), jnp.bfloat16),
-            jax.ShapeDtypeStruct((16, b_encoder.shape[0]), jnp.float32),
+    operands = (forcing, tile_weight.T, tile_part.T, tile_slot.T, initial_flow.T)
+    send = pl.pallas_call(
+        functools.partial(pack_kernel, basin_local),
+        out_shape=jax.ShapeDtypeStruct(
+            (part_count, tile_local + tile_local // 2 + EXTRAS, LANES), jnp.bfloat16
         ),
-        in_specs=[vmem] * 7 + [(vmem,) * len(tables)],
-        out_specs=(vmem, vmem),
-        compiler_params=params,
-    )(
-        jnp.swapaxes(forcing, 0, 1),
-        tile_part.T,
-        tile_slot.T,
-        tile_weight.T,
-        initial_flow.T,
-        b_encoder[None],
-        b_decoder[None],
-        tables,
-    )
+        in_specs=[pl.BlockSpec(memory_space=pltpu.HBM)] * len(operands),
+        out_specs=vmem,
+        scratch_shapes=[pltpu.VMEM(x.shape, x.dtype) for x in operands]
+        + [pltpu.SemaphoreType.DMA((len(operands),))],
+        compiler_params=pltpu.CompilerParams(vmem_limit_bytes=60 << 20),
+    )(*operands)
     arrived = lax.all_to_all(send, "basin", split_axis=0, concat_axis=0, tiled=True)
     sources = min(part_count, 8)
+    units = w_encoder.shape[0]
+    scale = jnp.where(jnp.arange(4 * units) // units == 2, 1.0, 0.5).astype(jnp.float32)
+    shared = (b_encoder[None] * scale, b_decoder[None] * scale, w_output[None], *tables)
+    blank = jnp.zeros((INPUT_ROW - sum(x.shape[0] for x in shared), 1), jnp.float32)
+    small = stacked(INPUT_ROW + FEAT, 4 * units, (*shared, blank, w_input * scale))
+    w_encoder = (w_encoder * scale).astype(jnp.bfloat16)
+    w_decoder = (w_decoder * scale).astype(jnp.bfloat16)
     lateral = pl.pallas_call(
         functools.partial(lstm_kernel, (hour_feat, tile_local, basin_local, groups, sources)),
         out_shape=jax.ShapeDtypeStruct((8, rows), jnp.float32),
-        in_specs=[vmem] * 6,
+        in_specs=[vmem] * 4,
         out_specs=vmem,
         compiler_params=params,
-    )(
-        arrived,
-        w_input,
-        w_encoder,
-        w_decoder,
-        jnp.broadcast_to(w_output[None], (8, w_output.shape[0])),
-        small,
-    )
+    )(arrived, small, w_encoder, w_decoder)
     axes = ("member", "basin")
     world = lax.axis_size("member") * part_count
     copies = jnp.broadcast_to(lateral[None], (world,) + lateral.shape)

time: 47.8 us -> 40.3 us (0.84)
  blocking collectives: 26.4 us -> 10.9 us
  local copies, waits for them, and re-layouts: 9.52 us -> 0.69 us
  starting transfers between devices: 0 us -> 7.29 us
  other arithmetic: 0 us -> 4.44 us
  waiting for transfers between devices: 0 us -> 3.3 us
  Pallas kernels: 10.6 us -> 12.5 us
    all_to_all x1 -> x0, blocking collectives: 15.5 us -> none  [on_device(): lax.all_to_all(send, 'basin', split_axis=0, concat_axis=0, tiled=True)]
    unnamed x29 -> x4, local copies, waits for them, and re-layouts: 9.49 us -> 0.01 us
    all_to_all x0 -> x1, starting transfers between devices: none -> 7.29 us  [on_device(): lax.all_to_all(send, 'basin', split_axis=0, concat_axis=0, tiled=True)]
    all_to_all x0 -> x1, waiting for transfers between devices: none -> 3.3 us  [on_device(): lax.all_to_all(send, 'basin', split_axis=0, concat_axis=0, tiled=True)]
    mul x0 -> x3, other arithmetic: none -> 2.11 us  [the longest x1 0.72 us: on_device(): w_input * scale]
    pallas_call x1, Pallas kernels: 0.1 us -> 1.98 us  [on_device(): pl.pallas_call(functools.partial(pack_kernel, basin_local), out_shape=jax...]
    convert_element_type x0 -> x3, other arithmetic: none -> 1.61 us  [the longest x2 1.37 us: stacked(): rows.astype(jnp.float32)]
    add x0 -> x1, other arithmetic: none -> 0.72 us  [stacked(): total + jnp.pad(rows.astype(jnp.float32), ((at, height - at - count), (0,...]
  transfers between devices with their start and end apart: 0 -> 1, of which waited for: 0 -> 1; matrix products, arithmetic and copies ran while one was open for 0% -> 13% of each run, Pallas kernels for 0% -> 0%
where the time goes in v3:
time: 40.3 us; the launch traced here: 39.8 us
  Pallas kernels  12.5 us (31%)
  blocking collectives  10.9 us (27%)
  starting transfers between devices  7.29 us (18%)
  other arithmetic  4.44 us (11%)
  waiting for transfers between devices  3.3 us (8%)
  between operations  0.7 us (2%)
  local copies, waits for them, and re-layouts  0.69 us (2%)
    all_to_all x1, blocking collectives, on_device(): lax.all_to_all(copies, axes, split_axis=0, concat_axis=0, tiled=True)  10.9 us
    pallas_call x1, Pallas kernels, on_device(): pl.pallas_call(functools.partial(lstm_kernel, (hour_feat, tile_local, bas...  7.71 us
    all_to_all x1, starting transfers between devices, on_device(): lax.all_to_all(send, 'basin', split_axis=0, concat_axis=0, tiled=True)  7.29 us
    all_to_all x1, waiting for transfers between devices, on_device(): lax.all_to_all(send, 'basin', split_axis=0, concat_axis=0, tiled=True)  3.3 us
    pallas_call x1, Pallas kernels, on_device(): pl.pallas_call(functools.partial(route_kernel, mem_local, basin_local, re...  2.79 us
    pallas_call x1, Pallas kernels, on_device(): pl.pallas_call(functools.partial(pack_kernel, basin_local), out_shape=jax...  1.98 us
    convert_element_type x2, other arithmetic, stacked(): rows.astype(jnp.float32)  1.37 us
  transfers between devices with their start and end apart: 1, of which 1 were waited for; matrix products, arithmetic and copies ran while one was open for 13% of the time, Pallas kernels for 0%

profile of v3, /device:TPU:0, one launch (start us, length us, event | category | flops | bytes accessed | tf_op | source)
XLA Modules:
  0.0 39.8 jit_solution(11332763023114618164)
XLA Ops:
  0.6 0.0 copy-start
  0.6 0.0 copy-start.1
  0.7 2.0 %shard_map.158 = bf16[8,112,128]{2,1,0:T(8,128)(2,1)} custom-call(bf16[64,4,192]{2,1,0:T(4,128)(2,1)} %refs_0_.1, f32[2,64]{1,0:T(2,128)} %bitcast.19, s32[2,64]{1,0:T(2,128)} %bitcast.20, s32[2,64]{1,0:T(2,128)} %bitcast.21, f32[4,32]{1,0:T(4,128)} %bitcast.18), custom_call_target="tpu_custom_call" | custom-call | tf_op jit(solution)/shard_map/pallas_call | solution.py:302
  2.6 7.3 %all-to-all-start = ((bf16[8,112,128]{2,1,0:T(8,128)(2,1)}), bf16[8,112,128]{2,1,0:T(8,128)(2,1)S(1)}, u32[]{:S(2)}, u32[]{:S(2)}) async-start(bf16[8,112,128]{2,1,0:T(8,128)(2,1)} %shard_map.158), calls=%async_computation | async-start | bytes 458752 | tf_op jit(solution)/shard_map/all_to_all | solution.py:313
  9.9 0.7 %fusion.6 = f32[1024]{0:T(1024)S(1)} fusion(f32[1024]{0:T(1024)} %param.21), kind=kLoop, calls=%fused_computation.15 | loop fusion | flops 11264 | bytes 8192 | tf_op jit(solution)/shard_map/mul | solution.py:317
  10.6 0.7 %fusion.5 = f32[1024]{0:T(1024)S(1)} fusion(f32[1024]{0:T(1024)} %param.23), kind=kLoop, calls=%fused_computation.14 | loop fusion | flops 11264 | bytes 8192 | tf_op jit(solution)/shard_map/mul | solution.py:317
  11.3 0.7 %convert_multiply_fusion = f32[8,1024]{1,0:T(8,128)S(1)} fusion(bf16[8,1024]{1,0:T(8,128)(2,1)} %param.19, f32[1024]{0:T(1024)S(1)} %fusion.4), kind=kLoop, calls=%fused_computation.3 | loop fusion | flops 16384 | bytes 53248 | tf_op jit(solution)/shard_map/mul | solution.py:319
  12.0 0.7 %convert_bitcast_fusion = f32[4,256]{1,0:T(4,128)S(1)} fusion(s32[256,4]{0,1:T(4,128)} %param.29), kind=kLoop, calls=%fused_computation.11 | loop fusion | flops 1024 | bytes 8192 | tf_op jit(solution)/shard_map/convert_element_type | solution.py:41
  12.7 0.7 %convert_element_type.49 = bf16[1,256]{1,0:T(2,128)(2,1)S(1)} reshape(bf16[256]{0:T(256)(128)(2,1)} %param.24) | data formatting | bytes 1024 | tf_op jit(solution)/shard_map/convert_element_type | solution.py:41
  13.4 0.7 %convert_element_type.50 = f32[256]{0:T(256)S(1)} convert(s32[256]{0:T(256)} %param.28) | non-fusion elementwise | flops 256 | bytes 2048 | tf_op jit(solution)/shard_map/convert_element_type | solution.py:41
  14.1 0.7 %pad_add_fusion.small = f32[24,1024]{1,0:T(8,128)S(1)} fusion(f32[8,1024]{1,0:T(8,128)S(1)} %convert_multiply_fusion, f32[6,1]{1,0:T(8,128)S(1)} %broadcast.65, f32[4,256]{1,0:T(4,128)S(1)} %convert_bitcast_fusion, f32[1,256]{1,0:T(1,128)S(1)} %bitcast.17, f32[1,256]{1,0:T(1,128)} %bitcast.22, f32[1,256]{1,0:T(1,128)} %bitcast.23, f32[1,1024]{1,0:T(1,128)S(1)} %bitcast.16, ...), kind=kLoop, calls=%fused_computation.2 | loop fusion | flops 221184 | bytes 146968 | tf_op jit(solution)/shard_map/add | solution.py:40
  14.8 0.0 copy-done
  14.8 0.0 copy-done.1
  14.8 0.2 multiply_convert_fusion
  15.1 3.3 %all-to-all-done.arrived = bf16[8,112,128]{2,1,0:T(8,128)(2,1)S(1)} async-done(((bf16[8,112,128]{2,1,0:T(8,128)(2,1)}), bf16[8,112,128]{2,1,0:T(8,128)(2,1)S(1)}, u32[]{:S(2)}, u32[]{:S(2)}) %all-to-all-start) | async-done | bytes 229408 | tf_op jit(solution)/shard_map/all_to_all | solution.py:313
  18.4 7.7 %shard_map.159 = f32[8,128]{1,0:T(8,128)S(1)} custom-call(bf16[8,112,128]{2,1,0:T(8,128)(2,1)S(1)} %all-to-all-done.arrived, f32[24,1024]{1,0:T(8,128)S(1)} %pad_add_fusion.small, bf16[256,1024]{1,0:T(8,128)(2,1)S(1)} %get-tuple-element.7.w_encoder, bf16[256,1024]{1,0:T(8,128)(2,1)S(1)} %get-tuple-element.6.w_decoder), custom_call_target="tpu_custom_call" | custom-call | tf_op jit(solution)/shard_map/pallas_call | solution.py:322
  26.1 10.9 %all_to_all.10 = f32[32,8,128]{2,1,0:T(8,128)S(1)} all-to-all(f32[32,8,128]{2,1,0:T(8,128)S(1)} %broadcast_in_dim.18), channel_id=1, replica_groups=mesh['basin'=8,'member'=4] {'member','basin'}, dimensions={0} | all-to-all | bytes 262144 | tf_op jit(solution)/shard_map/all_to_all | solution.py:332
  37.0 2.8 %shard_map.160 = (f32[6,4,32]{2,1,0:T(4,128)}, f32[6,32]{1,0:T(8,128)}) custom-call(f32[256,128]{1,0:T(8,128)S(1)} %bitcast.14, f32[24,1024]{1,0:T(8,128)S(1)} %pad_add_fusion.small), custom_call_target="tpu_custom_call" | custom-call | tf_op jit(solution)/shard_map/pallas_call | solution.py:335
  (3 shorter events, 0.0 us)
Async XLA Ops:
  0.6 14.2 %copy-start = (bf16[256,1024]{1,0:T(8,128)(2,1)S(1)}, bf16[256,1024]{1,0:T(8,128)(2,1)}, u32[]{:S(2)}) copy-start(bf16[256,1024]{1,0:T(8,128)(2,1)} %param.22) | copy-start | bytes 1572868
  0.6 14.2 %copy-start.1 = (bf16[256,1024]{1,0:T(8,128)(2,1)S(1)}, bf16[256,1024]{1,0:T(8,128)(2,1)}, u32[]{:S(2)}) copy-start(bf16[256,1024]{1,0:T(8,128)(2,1)} %param.20) | copy-start | bytes 1572868
  2.6 15.7 %all-to-all-start = ((bf16[8,112,128]{2,1,0:T(8,128)(2,1)}), bf16[8,112,128]{2,1,0:T(8,128)(2,1)S(1)}, u32[]{:S(2)}, u32[]{:S(2)}) async-start(bf16[8,112,128]{2,1,0:T(8,128)(2,1)} %shard_map.158), calls=%async_computation | async-start | bytes 458752 | tf_op jit(solution)/shard_map/all_to_all | solution.py:313

commit v4 on v3

--- a/solution.py
+++ b/solution.py
@@ -24,10 +24,11 @@
 def cell_update(gate_sum, memory_cell):
     units = memory_cell.shape[-1]
     input_gate = 0.5 * jnp.tanh(gate_sum[:, :units]) + 0.5
-    forget_gate = 0.5 * jnp.tanh(gate_sum[:, units : 2 * units]) + 0.5
     candidate = jnp.tanh(gate_sum[:, 2 * units : 3 * units])
+    kept = 0.5 * memory_cell
+    fresh = kept + input_gate * candidate
+    memory_cell = jnp.tanh(gate_sum[:, units : 2 * units]) * kept + fresh
     output_gate = 0.5 * jnp.tanh(gate_sum[:, 3 * units :]) + 0.5
-    memory_cell = forget_gate * memory_cell + input_gate * candidate
     hidden = (output_gate * jnp.tanh(memory_cell)).astype(jnp.bfloat16)
     return hidden, memory_cell
 
@@ -139,9 +140,11 @@
 
     hidden = jnp.zeros((rows, units), jnp.bfloat16)
     memory_cell = jnp.zeros((rows, units), jnp.float32)
+    ahead = dot(inputs[:, :FEAT], w_input) + b_encoder
     for hour in range(hours):
-        gate_sum = dot(inputs[:, hour * FEAT : (hour + 1) * FEAT], w_input) + b_encoder
-        gate_sum = gate_sum + dot(hidden, w_encoder[...])
+        gate_sum = ahead + dot(hidden, w_encoder[...]) if hour else ahead
+        if hour + 1 < hours:
+            ahead = dot(inputs[:, (hour + 1) * FEAT : (hour + 2) * FEAT], w_input) + b_encoder
         hidden, memory_cell = cell_update(gate_sum, memory_cell)
     for hour in range(DEC):
         gate_sum = dot(hidden, w_decoder[...]) + b_decoder
@@ -163,12 +166,39 @@
     halves = reaches // LANES
     per_member = halves * 8
     members = gathered.shape[0] // per_member
-    levels = jnp.broadcast_to(level_row, (members, reaches)).astype(jnp.int32)
-    source = lax.broadcasted_iota(jnp.int32, (reaches, reaches), 0).astype(jnp.float32)
-    links = jnp.zeros((reaches, reaches), jnp.float32)
+    shape = (members, LANES)
+
+    def spread(row):
+        return [jnp.broadcast_to(row[:, h * LANES : (h + 1) * LANES], shape) for h in range(halves)]
+
+    def pick(parts, index):
+        out = None
+        for h, part in enumerate(parts):
+            value = jnp.take_along_axis(part, index % LANES, axis=1)
+            out = value if out is None else jnp.where(index // LANES == h, value, out)
+        return out
+
+    level_parts = spread(level_row.astype(jnp.int32))
+    levels = jnp.concatenate(level_parts, axis=1)
+    sources, lags = [], []
     for entry in range(upstream.shape[0]):
-        links = links + jnp.where(source == upstream[entry : entry + 1, :], 1.0, 0.0)
-    links = links.astype(jnp.bfloat16)
+        named = spread(upstream[entry : entry + 1, :].astype(jnp.int32))
+        index = [jnp.maximum(x, 0) for x in named]
+        sources.append(index)
+        lags.append(
+            [jnp.where(x < 0, 0, level - pick(level_parts, i)) for x, level, i in zip(named, level_parts, index, strict=True)]
+        )
+
+    def handed_on(flow):
+        parts = [flow[:, h * LANES : (h + 1) * LANES] for h in range(halves)]
+        sums = [[jnp.zeros(shape, jnp.float32)] * halves for _ in range(LEVELS - 1)]
+        for index, lag in zip(sources, lags, strict=True):
+            for h in range(halves):
+                value = pick(parts, index[h])
+                for k in range(LEVELS - 1):
+                    sums[k][h] = sums[k][h] + jnp.where(lag[h] == k + 1, value, 0.0)
+        return [jnp.concatenate(x, axis=1) for x in sums]
+
     speed_rate = jnp.broadcast_to(celerity, (members, reaches))
     store_rate = jnp.broadcast_to(storage, (members, reaches))
 
@@ -181,28 +211,16 @@
     current = row(DEC)
     powered = power(current)
     series = [jnp.zeros((members, reaches), jnp.float32) for _ in range(DEC)]
+    given = []
     for step in range(DEC + LEVELS - 1):
-        target = jnp.zeros((members, reaches), jnp.float32)
-        parts, owners = [], []
+        target = store_rate * powered
         for level in range(LEVELS):
             hour = step - level
             if 0 <= hour < DEC:
-                target = jnp.where(levels == level, lateral[hour], target)
-                if level:
-                    flow = series[hour]
-                    for _ in range(3):
-                        piece = flow.astype(jnp.bfloat16)
-                        parts.append(piece)
-                        flow = flow - piece.astype(jnp.float32)
-                    owners.append(level)
-        if parts:
-            sums = dot(jnp.concatenate(parts, axis=0), links)
-            for i, level in enumerate(owners):
-                at = 3 * i * members
-                inflow = sums[at : at + members] + sums[at + members : at + 2 * members]
-                inflow = inflow + sums[at + 2 * members : at + 3 * members]
-                target = jnp.where(levels == level, target + speed_rate * inflow, target)
-        target = target + store_rate * powered
+                target = jnp.where(levels == level, target + lateral[hour], target)
+        for k in range(LEVELS - 1):
+            if step - 1 - k >= 0:
+                target = target + speed_rate * given[step - 1 - k][k]
         flow, flow_power = current, powered
         for _ in range(NEWTON):
             ratio = (target - (1.0 - BETA) * store_rate * flow_power) / (
@@ -213,6 +231,7 @@
         active = (levels <= step) & (levels > step - DEC)
         current = jnp.where(active, flow, current)
         powered = jnp.where(active, flow_power, powered)
+        given.append(handed_on(current) if step + 1 < DEC + LEVELS - 1 else None)
         for level in range(LEVELS):
             hour = step - level
             if 0 <= hour < DEC:

time: 40.3 us -> 39.3 us (0.975)
  Pallas kernels: 12.5 us -> 11.5 us
    pallas_call x1, Pallas kernels: 7.71 us -> 7.08 us  [on_device(): pl.pallas_call(functools.partial(lstm_kernel, (hour_feat, tile_local, bas...]
where the time goes in v4:
time: 39.3 us; the launch traced here: 38.9 us
  Pallas kernels  11.5 us (29%)
  blocking collectives  10.9 us (28%)
  starting transfers between devices  7.29 us (19%)
  other arithmetic  4.44 us (11%)
  waiting for transfers between devices  3.3 us (8%)
  between operations  0.7 us (2%)
  local copies, waits for them, and re-layouts  0.69 us (2%)
    all_to_all x1, blocking collectives, on_device(): lax.all_to_all(copies, axes, split_axis=0, concat_axis=0, tiled=True)  10.9 us
    all_to_all x1, starting transfers between devices, on_device(): lax.all_to_all(send, 'basin', split_axis=0, concat_axis=0, tiled=True)  7.29 us
    pallas_call x1, Pallas kernels, on_device(): pl.pallas_call(functools.partial(lstm_kernel, (hour_feat, tile_local, bas...  7.08 us
    all_to_all x1, waiting for transfers between devices, on_device(): lax.all_to_all(send, 'basin', split_axis=0, concat_axis=0, tiled=True)  3.3 us
    pallas_call x1, Pallas kernels, on_device(): pl.pallas_call(functools.partial(route_kernel, mem_local, basin_local, re...  2.45 us
    pallas_call x1, Pallas kernels, on_device(): pl.pallas_call(functools.partial(pack_kernel, basin_local), out_shape=jax...  1.98 us
    convert_element_type x2, other arithmetic, stacked(): rows.astype(jnp.float32)  1.37 us
  transfers between devices with their start and end apart: 1, of which 1 were waited for; matrix products, arithmetic and copies ran while one was open for 13% of the time, Pallas kernels for 0%

profile of v4, /device:TPU:0, one launch (start us, length us, event | category | flops | bytes accessed | tf_op | source)
XLA Modules:
  0.0 38.9 jit_solution(9658116106966154590)
XLA Ops:
  0.6 0.0 copy-start
  0.6 0.0 copy-start.1
  0.7 2.0 %shard_map.158 = bf16[8,112,128]{2,1,0:T(8,128)(2,1)} custom-call(bf16[64,4,192]{2,1,0:T(4,128)(2,1)} %refs_0_.1, f32[2,64]{1,0:T(2,128)} %bitcast.19, s32[2,64]{1,0:T(2,128)} %bitcast.20, s32[2,64]{1,0:T(2,128)} %bitcast.21, f32[4,32]{1,0:T(4,128)} %bitcast.18), custom_call_target="tpu_custom_call" | custom-call | tf_op jit(solution)/shard_map/pallas_call | solution.py:321
  2.6 7.3 %all-to-all-start = ((bf16[8,112,128]{2,1,0:T(8,128)(2,1)}), bf16[8,112,128]{2,1,0:T(8,128)(2,1)S(1)}, u32[]{:S(2)}, u32[]{:S(2)}) async-start(bf16[8,112,128]{2,1,0:T(8,128)(2,1)} %shard_map.158), calls=%async_computation | async-start | bytes 458752 | tf_op jit(solution)/shard_map/all_to_all | solution.py:332
  9.9 0.7 %fusion.6 = f32[1024]{0:T(1024)S(1)} fusion(f32[1024]{0:T(1024)} %param.21), kind=kLoop, calls=%fused_computation.15 | loop fusion | flops 11264 | bytes 8192 | tf_op jit(solution)/shard_map/mul | solution.py:336
  10.6 0.7 %fusion.5 = f32[1024]{0:T(1024)S(1)} fusion(f32[1024]{0:T(1024)} %param.23), kind=kLoop, calls=%fused_computation.14 | loop fusion | flops 11264 | bytes 8192 | tf_op jit(solution)/shard_map/mul | solution.py:336
  11.3 0.7 %convert_multiply_fusion = f32[8,1024]{1,0:T(8,128)S(1)} fusion(bf16[8,1024]{1,0:T(8,128)(2,1)} %param.19, f32[1024]{0:T(1024)S(1)} %fusion.4), kind=kLoop, calls=%fused_computation.3 | loop fusion | flops 16384 | bytes 53248 | tf_op jit(solution)/shard_map/mul | solution.py:338
  12.0 0.7 %convert_bitcast_fusion = f32[4,256]{1,0:T(4,128)S(1)} fusion(s32[256,4]{0,1:T(4,128)} %param.29), kind=kLoop, calls=%fused_computation.11 | loop fusion | flops 1024 | bytes 8192 | tf_op jit(solution)/shard_map/convert_element_type | solution.py:42
  12.7 0.7 %convert_element_type.49 = bf16[1,256]{1,0:T(2,128)(2,1)S(1)} reshape(bf16[256]{0:T(256)(128)(2,1)} %param.24) | data formatting | bytes 1024 | tf_op jit(solution)/shard_map/convert_element_type | solution.py:42
  13.4 0.7 %convert_element_type.50 = f32[256]{0:T(256)S(1)} convert(s32[256]{0:T(256)} %param.28) | non-fusion elementwise | flops 256 | bytes 2048 | tf_op jit(solution)/shard_map/convert_element_type | solution.py:42
  14.1 0.7 %pad_add_fusion.small = f32[24,1024]{1,0:T(8,128)S(1)} fusion(f32[8,1024]{1,0:T(8,128)S(1)} %convert_multiply_fusion, f32[6,1]{1,0:T(8,128)S(1)} %broadcast.65, f32[4,256]{1,0:T(4,128)S(1)} %convert_bitcast_fusion, f32[1,256]{1,0:T(1,128)S(1)} %bitcast.17, f32[1,256]{1,0:T(1,128)} %bitcast.22, f32[1,256]{1,0:T(1,128)} %bitcast.23, f32[1,1024]{1,0:T(1,128)S(1)} %bitcast.16, ...), kind=kLoop, calls=%fused_computation.2 | loop fusion | flops 221184 | bytes 146968 | tf_op jit(solution)/shard_map/add | solution.py:41
  14.8 0.0 copy-done
  14.8 0.0 copy-done.1
  14.8 0.2 multiply_convert_fusion
  15.1 3.3 %all-to-all-done.arrived = bf16[8,112,128]{2,1,0:T(8,128)(2,1)S(1)} async-done(((bf16[8,112,128]{2,1,0:T(8,128)(2,1)}), bf16[8,112,128]{2,1,0:T(8,128)(2,1)S(1)}, u32[]{:S(2)}, u32[]{:S(2)}) %all-to-all-start) | async-done | bytes 229408 | tf_op jit(solution)/shard_map/all_to_all | solution.py:332
  18.4 7.1 %shard_map.159 = f32[8,128]{1,0:T(8,128)S(1)} custom-call(bf16[8,112,128]{2,1,0:T(8,128)(2,1)S(1)} %all-to-all-done.arrived, f32[24,1024]{1,0:T(8,128)S(1)} %pad_add_fusion.small, bf16[256,1024]{1,0:T(8,128)(2,1)S(1)} %get-tuple-element.7.w_encoder, bf16[256,1024]{1,0:T(8,128)(2,1)S(1)} %get-tuple-element.6.w_decoder), custom_call_target="tpu_custom_call" | custom-call | tf_op jit(solution)/shard_map/pallas_call | solution.py:341
  25.5 10.9 %all_to_all.10 = f32[32,8,128]{2,1,0:T(8,128)S(1)} all-to-all(f32[32,8,128]{2,1,0:T(8,128)S(1)} %broadcast_in_dim.18), channel_id=1, replica_groups=mesh['basin'=8,'member'=4] {'member','basin'}, dimensions={0} | all-to-all | bytes 262144 | tf_op jit(solution)/shard_map/all_to_all | solution.py:351
  36.4 2.5 %shard_map.160 = (f32[6,4,32]{2,1,0:T(4,128)}, f32[6,32]{1,0:T(8,128)}) custom-call(f32[256,128]{1,0:T(8,128)S(1)} %bitcast.14, f32[24,1024]{1,0:T(8,128)S(1)} %pad_add_fusion.small), custom_call_target="tpu_custom_call" | custom-call | tf_op jit(solution)/shard_map/pallas_call | solution.py:354
  (3 shorter events, 0.0 us)
Async XLA Ops:
  0.6 14.2 %copy-start = (bf16[256,1024]{1,0:T(8,128)(2,1)S(1)}, bf16[256,1024]{1,0:T(8,128)(2,1)}, u32[]{:S(2)}) copy-start(bf16[256,1024]{1,0:T(8,128)(2,1)} %param.22) | copy-start | bytes 1572868
  0.6 14.2 %copy-start.1 = (bf16[256,1024]{1,0:T(8,128)(2,1)S(1)}, bf16[256,1024]{1,0:T(8,128)(2,1)}, u32[]{:S(2)}) copy-start(bf16[256,1024]{1,0:T(8,128)(2,1)} %param.20) | copy-start | bytes 1572868
  2.6 15.7 %all-to-all-start = ((bf16[8,112,128]{2,1,0:T(8,128)(2,1)}), bf16[8,112,128]{2,1,0:T(8,128)(2,1)S(1)}, u32[]{:S(2)}, u32[]{:S(2)}) async-start(bf16[8,112,128]{2,1,0:T(8,128)(2,1)} %shard_map.158), calls=%async_computation | async-start | bytes 458752 | tf_op jit(solution)/shard_map/all_to_all | solution.py:332

commit v5 on v4

--- a/solution.py
+++ b/solution.py
@@ -15,7 +15,9 @@
 BETA = 0.6
 LANES = 128
 KERNEL_REACHES = 512
-EXTRAS = 16
+EXTRAS = 8
+CARRIED = jnp.float16
+HALF_STEP = 2.0**11
 INPUT_ROW = 16
 
 dot = functools.partial(jnp.dot, preferred_element_type=jnp.float32)
@@ -82,13 +84,33 @@
         own_flow = flow[member : member + 1, :]
         own_flow = jnp.concatenate([own_flow] * owners, axis=1)
         rows = common + pieces(jnp.where(mine, own_flow, 0.0))
-        rows.append(jnp.zeros((EXTRAS - len(rows), LANES), jnp.float32))
         extras = jnp.concatenate(rows, axis=0).astype(jnp.bfloat16)
         for group in range(groups):
             device = member * groups + group
             send[device, :tile_local, :] = first
             send[device, tile_local : tile_local + half, :] = second
             send[device, tile_local + half :, :] = extras
+
+
+def encode(values):
+    spread = values * (2.0**13 + 1.0)
+    rounded = spread - (spread - values)
+    place = (values - rounded) / jnp.maximum(rounded, 1e-30)
+    digits = jnp.clip(jnp.floor(place * (1.5 * HALF_STEP) + 0.5), -1.0, 1.0)
+    total = digits[0:1]
+    for k in range(1, values.shape[0]):
+        total = total + 3.0**k * digits[k : k + 1]
+    return jnp.concatenate([rounded, total], axis=0)
+
+
+def decode(rows):
+    *rounded, total = rows
+    values = []
+    for row in rounded:
+        above = jnp.floor(total * (1.0 / 3.0) + 0.5)
+        values.append(row + row * ((total - 3.0 * above) * (1.0 / (1.5 * HALF_STEP))))
+        total = above
+    return values
 
 
 def lstm_kernel(
@@ -132,8 +154,7 @@
     owners = rows // basin_local
     flow = arrived[pl.ds(half * owners, owners), extra_at:, :].astype(jnp.float32)
     flow = jnp.sum(flow, axis=0)
-    out[DEC : DEC + 1, :] = flow[5:6] + flow[6:7] + flow[7:8]
-    out[DEC + 1 :, :] = jnp.zeros((out.shape[0] - DEC - 1, rows), jnp.float32)
+    results = []
     b_encoder, b_decoder = small[0:1, : 4 * units], small[1:2, : 4 * units]
     w_input = small[INPUT_ROW : INPUT_ROW + FEAT, : 4 * units].astype(jnp.bfloat16)
     w_output = jnp.broadcast_to(small[2:3, :units], (8, units)).astype(jnp.bfloat16)
@@ -153,7 +174,9 @@
             w_output, hidden, (((1,), (1,)), ((), ())), preferred_element_type=jnp.float32
         )[0:1]
         runoff = jnp.maximum(runoff, 0.0) + jnp.log(1.0 + jnp.exp(-jnp.abs(runoff)))
-        out[hour : hour + 1, :] = runoff
+        results.append(runoff)
+    results.append(flow[5:6] + flow[6:7] + flow[7:8])
+    out[...] = encode(jnp.concatenate(results, axis=0))
 
 
 def power(flow):
@@ -207,8 +230,7 @@
             [gathered[pl.ds(h * 8 + k, members, stride=per_member), :] for h in range(halves)], axis=1
         )
 
-    lateral = [row(k) for k in range(DEC)]
-    current = row(DEC)
+    *lateral, current = decode([row(k) for k in range(8)])
     powered = power(current)
     series = [jnp.zeros((members, reaches), jnp.float32) for _ in range(DEC)]
     given = []
@@ -259,7 +281,8 @@
     members = gathered.shape[0] * gathered.shape[2] // reaches
     whole = gathered.reshape(members, -1, gathered.shape[1], gathered.shape[2])
     whole = jnp.transpose(whole, (1, 3, 0, 2)).reshape(reaches, members, gathered.shape[1])
-    lateral, initial = whole[:, :, :DEC], whole[:, :, DEC]
+    *lateral, initial = decode([whole[:, :, k] for k in range(8)])
+    lateral = jnp.stack(lateral, axis=2)
     speed_rate, store_rate = celerity[:, None], storage[:, None]
     up_index = jnp.where(upstream < 0, reaches, upstream)
     outflow = jnp.zeros_like(lateral)
@@ -347,8 +370,9 @@
     )(arrived, small, w_encoder, w_decoder)
     axes = ("member", "basin")
     world = lax.axis_size("member") * part_count
-    copies = jnp.broadcast_to(lateral[None], (world,) + lateral.shape)
+    copies = jnp.broadcast_to(lateral.astype(CARRIED)[None], (world,) + lateral.shape)
     gathered = lax.all_to_all(copies, axes, split_axis=0, concat_axis=0, tiled=True)
+    gathered = gathered.astype(jnp.float32)
     if not in_kernel:
         return route_plain(gathered, upstream, reach_level, celerity, storage, mem_local, basin_local)
     discharge, ensemble = pl.pallas_call(

time: 39.3 us -> 38.7 us (0.985)
  other arithmetic: 4.44 us -> 1.35 us
  waiting for transfers between devices: 3.3 us -> 5.37 us
  local copies, waits for them, and re-layouts: 0.69 us -> 1.39 us
  blocking collectives: 10.9 us -> 10.4 us
    all_to_all x1, waiting for transfers between devices: 3.3 us -> 5.37 us  [on_device(): lax.all_to_all(send, 'basin', split_axis=0, concat_axis=0, tiled=True)]
    unnamed x4 -> x18, local copies, waits for them, and re-layouts: 0.01 us -> 1.37 us
    convert_element_type x2, other arithmetic: 1.37 us -> 0.01 us  [stacked(): rows.astype(jnp.float32)]
    convert_element_type x1, other arithmetic: 0.24 us -> 1.28 us  [on_device(): w_decoder = (w_decoder * scale).astype(jnp.bfloat16)]
    mul x1, other arithmetic: 0.72 us -> 0.01 us  [on_device(): w_input * scale]
    add x1, other arithmetic: 0.72 us -> 0.02 us  [stacked(): total + jnp.pad(rows.astype(jnp.float32), ((at, height - at - count), (0,...]
    mul x1, other arithmetic: 0.69 us -> 0.01 us  [on_device(): b_encoder[None] * scale]
    mul x1, other arithmetic: 0.69 us -> 0.01 us  [on_device(): b_decoder[None] * scale]
  transfers between devices with their start and end apart: 1 -> 1, of which waited for: 1 -> 1; matrix products, arithmetic and copies ran while one was open for 13% -> 4% of each run, Pallas kernels for 0% -> 0%
where the time goes in v5:
time: 38.7 us; the launch traced here: 38.3 us
  Pallas kernels  11.6 us (30%)
  blocking collectives  10.4 us (27%)
  starting transfers between devices  7.42 us (19%)
  waiting for transfers between devices  5.37 us (14%)
  local copies, waits for them, and re-layouts  1.39 us (4%)
  other arithmetic  1.35 us (3%)
  between operations  0.83 us (2%)
    all_to_all x1, blocking collectives, on_device(): lax.all_to_all(copies, axes, split_axis=0, concat_axis=0, tiled=True)  10.4 us
    all_to_all x1, starting transfers between devices, on_device(): lax.all_to_all(send, 'basin', split_axis=0, concat_axis=0, tiled=True)  7.42 us
    pallas_call x1, Pallas kernels, on_device(): pl.pallas_call(functools.partial(lstm_kernel, (hour_feat, tile_local, bas...  7.12 us
    all_to_all x1, waiting for transfers between devices, on_device(): lax.all_to_all(send, 'basin', split_axis=0, concat_axis=0, tiled=True)  5.37 us
    pallas_call x1, Pallas kernels, on_device(): pl.pallas_call(functools.partial(route_kernel, mem_local, basin_local, re...  2.48 us
    pallas_call x1, Pallas kernels, on_device(): pl.pallas_call(functools.partial(pack_kernel, basin_local), out_shape=jax...  1.96 us
    unnamed x18, local copies, waits for them, and re-layouts  1.37 us
    convert_element_type x1, other arithmetic, on_device(): w_decoder = (w_decoder * scale).astype(jnp.bfloat16)  1.28 us
  transfers between devices with their start and end apart: 1, of which 1 were waited for; matrix products, arithmetic and copies ran while one was open for 4% of the time, Pallas kernels for 0%

profile of v5, /device:TPU:0, one launch (start us, length us, event | category | flops | bytes accessed | tf_op | source)
XLA Modules:
  0.0 38.3 jit_solution(9596525197643867107)
XLA Ops:
  0.6 0.0 copy-start
  0.6 2.0 %shard_map.158 = bf16[8,104,128]{2,1,0:T(8,128)(2,1)} custom-call(bf16[64,4,192]{2,1,0:T(4,128)(2,1)} %refs_0_.1, f32[2,64]{1,0:T(2,128)} %bitcast.20, s32[2,64]{1,0:T(2,128)} %bitcast.21, s32[2,64]{1,0:T(2,128)} %bitcast.22, f32[4,32]{1,0:T(4,128)} %bitcast.19), custom_call_target="tpu_custom_call" | custom-call | tf_op jit(solution)/shard_map/pallas_call | solution.py:344
  2.6 0.0 copy-start.8
  2.6 0.0 copy-start.7
  2.6 0.0 copy-start.2
  2.6 0.0 copy-start.3
  2.7 7.4 %all-to-all-start = ((bf16[8,104,128]{2,1,0:T(8,128)(2,1)}), bf16[8,104,128]{2,1,0:T(8,128)(2,1)S(1)}, u32[]{:S(2)}, u32[]{:S(2)}) async-start(bf16[8,104,128]{2,1,0:T(8,128)(2,1)} %shard_map.158), calls=%async_computation | async-start | bytes 425984 | tf_op jit(solution)/shard_map/all_to_all | solution.py:355
  10.1 0.0 copy-start.1
  10.1 0.0 copy-done.8
  10.1 0.0 copy-done.7
  10.1 0.0 copy-done.2
  10.2 0.0 copy-done.3
  10.2 0.0 copy-start.4
  10.2 0.7 %copy-done.4 = s32[256,4]{0,1:T(4,128)S(1)} copy-done((s32[256,4]{0,1:T(4,128)S(1)}, s32[256,4]{0,1:T(4,128)}, u32[]{:S(2)}) %copy-start.4) | copy-done | bytes 4120
  10.9 0.0 copy-done.1
  10.9 0.0 copy-start.5
  10.9 0.0 copy-start.6
  10.9 0.6 %copy-done.5 = f32[256]{0:T(256)S(1)} copy-done((f32[256]{0:T(256)S(1)}, f32[256]{0:T(256)}, u32[]{:S(2)}) %copy-start.5) | copy-done | bytes 1048
  11.6 0.0 copy-done.6
  11.6 0.0 copy-done
  11.6 1.3 %multiply_convert_fusion = (bf16[256,1024]{1,0:T(8,128)(2,1)S(1)}, bf16[256,1024]{1,0:T(8,128)(2,1)S(1)}) fusion(bf16[256,1024]{1,0:T(8,128)(2,1)S(1)} %copy-done, f32[1024]{0:T(1024)S(1)} %fusion.4, bf16[256,1024]{1,0:T(8,128)(2,1)} %param.20), kind=kLoop, calls=%fused_computation | loop fusion | flops 1572864 | bytes 2101248 | tf_op jit(solution)/shard_map/convert_element_type | solution.py:363
  12.9 5.4 %all-to-all-done.arrived = bf16[8,104,128]{2,1,0:T(8,128)(2,1)S(1)} async-done(((bf16[8,104,128]{2,1,0:T(8,128)(2,1)}), bf16[8,104,128]{2,1,0:T(8,128)(2,1)S(1)}, u32[]{:S(2)}, u32[]{:S(2)}) %all-to-all-start) | async-done | bytes 213024 | tf_op jit(solution)/shard_map/all_to_all | solution.py:355
  18.3 7.1 %shard_map.159 = f32[8,128]{1,0:T(8,128)S(1)} custom-call(bf16[8,104,128]{2,1,0:T(8,128)(2,1)S(1)} %all-to-all-done.arrived, f32[24,1024]{1,0:T(8,128)S(1)} %pad_add_fusion.small, bf16[256,1024]{1,0:T(8,128)(2,1)S(1)} %get-tuple-element.7.w_encoder, bf16[256,1024]{1,0:T(8,128)(2,1)S(1)} %get-tuple-element.6.w_decoder), custom_call_target="tpu_custom_call" | custom-call | tf_op jit(solution)/shard_map/pallas_call | solution.py:364
  25.4 10.4 %all_to_all.10 = f16[32,8,128]{2,1,0:T(8,128)(2,1)S(1)} all-to-all(f16[32,8,128]{2,1,0:T(8,128)(2,1)S(1)} %broadcast_in_dim.18), channel_id=1, replica_groups=mesh['basin'=8,'member'=4] {'member','basin'}, dimensions={0} | all-to-all | bytes 131072 | tf_op jit(solution)/shard_map/all_to_all | solution.py:374
  35.8 2.5 %shard_map.160 = (f32[6,4,32]{2,1,0:T(4,128)}, f32[6,32]{1,0:T(8,128)}) custom-call(f32[256,128]{1,0:T(8,128)S(1)} %bitcast_convert_fusion.gathered, f32[24,1024]{1,0:T(8,128)S(1)} %pad_add_fusion.small), custom_call_target="tpu_custom_call" | custom-call | tf_op jit(solution)/shard_map/pallas_call | solution.py:378
  (12 shorter events, 0.1 us)
Async XLA Ops:
  0.6 11.0 %copy-start = (bf16[256,1024]{1,0:T(8,128)(2,1)S(1)}, bf16[256,1024]{1,0:T(8,128)(2,1)}, u32[]{:S(2)}) copy-start(bf16[256,1024]{1,0:T(8,128)(2,1)} %param.22) | copy-start | bytes 1572868
  2.6 7.5 %copy-start.8 = (bf16[256]{0:T(256)(128)(2,1)S(1)}, bf16[256]{0:T(256)(128)(2,1)}, u32[]{:S(2)}) copy-start(bf16[256]{0:T(256)(128)(2,1)} %param.24) | copy-start | bytes 1540
  2.6 7.5 %copy-start.7 = (s32[256]{0:T(256)S(1)}, s32[256]{0:T(256)}, u32[]{:S(2)}) copy-start(s32[256]{0:T(256)} %param.28) | copy-start | bytes 3076
  2.6 7.5 %copy-start.2 = (f32[1024]{0:T(1024)S(1)}, f32[1024]{0:T(1024)}, u32[]{:S(2)}) copy-start(f32[1024]{0:T(1024)} %param.21) | copy-start | bytes 12292
  2.6 7.5 %copy-start.3 = (f32[1024]{0:T(1024)S(1)}, f32[1024]{0:T(1024)}, u32[]{:S(2)}) copy-start(f32[1024]{0:T(1024)} %param.23) | copy-start | bytes 12292
  2.7 15.6 %all-to-all-start = ((bf16[8,104,128]{2,1,0:T(8,128)(2,1)}), bf16[8,104,128]{2,1,0:T(8,128)(2,1)S(1)}, u32[]{:S(2)}, u32[]{:S(2)}) async-start(bf16[8,104,128]{2,1,0:T(8,128)(2,1)} %shard_map.158), calls=%async_computation | async-start | bytes 425984 | tf_op jit(solution)/shard_map/all_to_all | solution.py:355
  10.1 0.8 %copy-start.1 = (bf16[8,1024]{1,0:T(8,128)(2,1)S(1)}, bf16[8,1024]{1,0:T(8,128)(2,1)}, u32[]{:S(2)}) copy-start(bf16[8,1024]{1,0:T(8,128)(2,1)} %param.19) | copy-start | bytes 49156
  10.2 0.7 %copy-start.4 = (s32[256,4]{0,1:T(4,128)S(1)}, s32[256,4]{0,1:T(4,128)}, u32[]{:S(2)}) copy-start(s32[256,4]{0,1:T(4,128)} %param.29) | copy-start | bytes 12292
  10.9 0.7 %copy-start.5 = (f32[256]{0:T(256)S(1)}, f32[256]{0:T(256)}, u32[]{:S(2)}) copy-start(f32[256]{0:T(256)} %param.26) | copy-start | bytes 3076
  10.9 0.7 %copy-start.6 = (f32[256]{0:T(256)S(1)}, f32[256]{0:T(256)}, u32[]{:S(2)}) copy-start(f32[256]{0:T(256)} %param.25) | copy-start | bytes 3076

commit v6 on v5

--- a/solution.py
+++ b/solution.py
@@ -167,14 +167,19 @@
         if hour + 1 < hours:
             ahead = dot(inputs[:, (hour + 1) * FEAT : (hour + 2) * FEAT], w_input) + b_encoder
         hidden, memory_cell = cell_update(gate_sum, memory_cell)
+
+    def runoff(state):
+        sums = lax.dot_general(
+            w_output, state, (((1,), (1,)), ((), ())), preferred_element_type=jnp.float32
+        )[0:1]
+        return jnp.maximum(sums, 0.0) + jnp.log(1.0 + jnp.exp(-jnp.abs(sums)))
+
     for hour in range(DEC):
         gate_sum = dot(hidden, w_decoder[...]) + b_decoder
+        if hour:
+            results.append(runoff(hidden))
         hidden, memory_cell = cell_update(gate_sum, memory_cell)
-        runoff = lax.dot_general(
-            w_output, hidden, (((1,), (1,)), ((), ())), preferred_element_type=jnp.float32
-        )[0:1]
-        runoff = jnp.maximum(runoff, 0.0) + jnp.log(1.0 + jnp.exp(-jnp.abs(runoff)))
-        results.append(runoff)
+    results.append(runoff(hidden))
     results.append(flow[5:6] + flow[6:7] + flow[7:8])
     out[...] = encode(jnp.concatenate(results, axis=0))
 
@@ -197,8 +202,8 @@
     def pick(parts, index):
         out = None
         for h, part in enumerate(parts):
-            value = jnp.take_along_axis(part, index % LANES, axis=1)
-            out = value if out is None else jnp.where(index // LANES == h, value, out)
+            value = jnp.take_along_axis(part, index & (LANES - 1), axis=1)
+            out = value if out is None else jnp.where(index >= h * LANES, value, out)
         return out
 
     level_parts = spread(level_row.astype(jnp.int32))
@@ -245,11 +250,10 @@
                 target = target + speed_rate * given[step - 1 - k][k]
         flow, flow_power = current, powered
         for _ in range(NEWTON):
-            ratio = (target - (1.0 - BETA) * store_rate * flow_power) / (
-                speed_rate * flow + BETA * store_rate * flow_power
-            )
-            flow = flow * jnp.maximum(ratio, 0.5)
-            flow_power = power(flow)
+            slope = speed_rate * flow + BETA * store_rate * flow_power
+            reached = jnp.maximum(target - (1.0 - BETA) * store_rate * flow_power, 0.5 * slope)
+            flow = flow * (reached / slope)
+            flow_power = flow_power * jnp.exp(BETA * (jnp.log(reached) - jnp.log(slope)))
         active = (levels <= step) & (levels > step - DEC)
         current = jnp.where(active, flow, current)
         powered = jnp.where(active, flow_power, powered)

time: 38.7 us -> 38.4 us (level)
  no operation moved by 1% of the time
where the time goes in v6:
time: 38.4 us; the launch traced here: 38 us
  Pallas kernels  11.3 us (29%)
  blocking collectives  10.4 us (27%)
  starting transfers between devices  7.42 us (19%)
  waiting for transfers between devices  5.37 us (14%)
  local copies, waits for them, and re-layouts  1.39 us (4%)
  other arithmetic  1.35 us (4%)
  between operations  0.83 us (2%)
    all_to_all x1, blocking collectives, on_device(): lax.all_to_all(copies, axes, split_axis=0, concat_axis=0, tiled=True)  10.4 us
    all_to_all x1, starting transfers between devices, on_device(): lax.all_to_all(send, 'basin', split_axis=0, concat_axis=0, tiled=True)  7.42 us
    pallas_call x1, Pallas kernels, on_device(): pl.pallas_call(functools.partial(lstm_kernel, (hour_feat, tile_local, bas...  6.97 us
    all_to_all x1, waiting for transfers between devices, on_device(): lax.all_to_all(send, 'basin', split_axis=0, concat_axis=0, tiled=True)  5.37 us
    pallas_call x1, Pallas kernels, on_device(): pl.pallas_call(functools.partial(route_kernel, mem_local, basin_local, re...  2.38 us
    pallas_call x1, Pallas kernels, on_device(): pl.pallas_call(functools.partial(pack_kernel, basin_local), out_shape=jax...  1.96 us
    unnamed x18, local copies, waits for them, and re-layouts  1.37 us
    convert_element_type x1, other arithmetic, on_device(): w_decoder = (w_decoder * scale).astype(jnp.bfloat16)  1.28 us
  transfers between devices with their start and end apart: 1, of which 1 were waited for; matrix products, arithmetic and copies ran while one was open for 4% of the time, Pallas kernels for 0%

profile of v6, /device:TPU:0, one launch (start us, length us, event | category | flops | bytes accessed | tf_op | source)
XLA Modules:
  0.0 38.0 jit_solution(3995808069265649886)
XLA Ops:
  0.6 0.0 copy-start
  0.6 2.0 %shard_map.158 = bf16[8,104,128]{2,1,0:T(8,128)(2,1)} custom-call(bf16[64,4,192]{2,1,0:T(4,128)(2,1)} %refs_0_.1, f32[2,64]{1,0:T(2,128)} %bitcast.20, s32[2,64]{1,0:T(2,128)} %bitcast.21, s32[2,64]{1,0:T(2,128)} %bitcast.22, f32[4,32]{1,0:T(4,128)} %bitcast.19), custom_call_target="tpu_custom_call" | custom-call | tf_op jit(solution)/shard_map/pallas_call | solution.py:348
  2.6 0.0 copy-start.8
  2.6 0.0 copy-start.7
  2.6 0.0 copy-start.2
  2.6 0.0 copy-start.3
  2.7 7.4 %all-to-all-start = ((bf16[8,104,128]{2,1,0:T(8,128)(2,1)}), bf16[8,104,128]{2,1,0:T(8,128)(2,1)S(1)}, u32[]{:S(2)}, u32[]{:S(2)}) async-start(bf16[8,104,128]{2,1,0:T(8,128)(2,1)} %shard_map.158), calls=%async_computation | async-start | bytes 425984 | tf_op jit(solution)/shard_map/all_to_all | solution.py:359
  10.1 0.0 copy-start.1
  10.1 0.0 copy-done.8
  10.1 0.0 copy-done.7
  10.1 0.0 copy-done.2
  10.2 0.0 copy-done.3
  10.2 0.0 copy-start.4
  10.2 0.7 %copy-done.4 = s32[256,4]{0,1:T(4,128)S(1)} copy-done((s32[256,4]{0,1:T(4,128)S(1)}, s32[256,4]{0,1:T(4,128)}, u32[]{:S(2)}) %copy-start.4) | copy-done | bytes 4120
  10.9 0.0 copy-done.1
  10.9 0.0 copy-start.5
  10.9 0.0 copy-start.6
  10.9 0.6 %copy-done.5 = f32[256]{0:T(256)S(1)} copy-done((f32[256]{0:T(256)S(1)}, f32[256]{0:T(256)}, u32[]{:S(2)}) %copy-start.5) | copy-done | bytes 1048
  11.6 0.0 copy-done.6
  11.6 0.0 copy-done
  11.6 1.3 %multiply_convert_fusion = (bf16[256,1024]{1,0:T(8,128)(2,1)S(1)}, bf16[256,1024]{1,0:T(8,128)(2,1)S(1)}) fusion(bf16[256,1024]{1,0:T(8,128)(2,1)S(1)} %copy-done, f32[1024]{0:T(1024)S(1)} %fusion.4, bf16[256,1024]{1,0:T(8,128)(2,1)} %param.20), kind=kLoop, calls=%fused_computation | loop fusion | flops 1572864 | bytes 2101248 | tf_op jit(solution)/shard_map/convert_element_type | solution.py:367
  12.9 5.4 %all-to-all-done.arrived = bf16[8,104,128]{2,1,0:T(8,128)(2,1)S(1)} async-done(((bf16[8,104,128]{2,1,0:T(8,128)(2,1)}), bf16[8,104,128]{2,1,0:T(8,128)(2,1)S(1)}, u32[]{:S(2)}, u32[]{:S(2)}) %all-to-all-start) | async-done | bytes 213024 | tf_op jit(solution)/shard_map/all_to_all | solution.py:359
  18.3 7.0 %shard_map.159 = f32[8,128]{1,0:T(8,128)S(1)} custom-call(bf16[8,104,128]{2,1,0:T(8,128)(2,1)S(1)} %all-to-all-done.arrived, f32[24,1024]{1,0:T(8,128)S(1)} %pad_add_fusion.small, bf16[256,1024]{1,0:T(8,128)(2,1)S(1)} %get-tuple-element.7.w_encoder, bf16[256,1024]{1,0:T(8,128)(2,1)S(1)} %get-tuple-element.6.w_decoder), custom_call_target="tpu_custom_call" | custom-call | tf_op jit(solution)/shard_map/pallas_call | solution.py:368
  25.3 10.4 %all_to_all.10 = f16[32,8,128]{2,1,0:T(8,128)(2,1)S(1)} all-to-all(f16[32,8,128]{2,1,0:T(8,128)(2,1)S(1)} %broadcast_in_dim.18), channel_id=1, replica_groups=mesh['basin'=8,'member'=4] {'member','basin'}, dimensions={0} | all-to-all | bytes 131072 | tf_op jit(solution)/shard_map/all_to_all | solution.py:378
  35.7 2.4 %shard_map.160 = (f32[6,4,32]{2,1,0:T(4,128)}, f32[6,32]{1,0:T(8,128)}) custom-call(f32[256,128]{1,0:T(8,128)S(1)} %bitcast_convert_fusion.gathered, f32[24,1024]{1,0:T(8,128)S(1)} %pad_add_fusion.small), custom_call_target="tpu_custom_call" | custom-call | tf_op jit(solution)/shard_map/pallas_call | solution.py:382
  (12 shorter events, 0.1 us)
Async XLA Ops:
  0.6 11.0 %copy-start = (bf16[256,1024]{1,0:T(8,128)(2,1)S(1)}, bf16[256,1024]{1,0:T(8,128)(2,1)}, u32[]{:S(2)}) copy-start(bf16[256,1024]{1,0:T(8,128)(2,1)} %param.22) | copy-start | bytes 1572868
  2.6 7.5 %copy-start.8 = (bf16[256]{0:T(256)(128)(2,1)S(1)}, bf16[256]{0:T(256)(128)(2,1)}, u32[]{:S(2)}) copy-start(bf16[256]{0:T(256)(128)(2,1)} %param.24) | copy-start | bytes 1540
  2.6 7.5 %copy-start.7 = (s32[256]{0:T(256)S(1)}, s32[256]{0:T(256)}, u32[]{:S(2)}) copy-start(s32[256]{0:T(256)} %param.28) | copy-start | bytes 3076
  2.6 7.5 %copy-start.2 = (f32[1024]{0:T(1024)S(1)}, f32[1024]{0:T(1024)}, u32[]{:S(2)}) copy-start(f32[1024]{0:T(1024)} %param.21) | copy-start | bytes 12292
  2.6 7.5 %copy-start.3 = (f32[1024]{0:T(1024)S(1)}, f32[1024]{0:T(1024)}, u32[]{:S(2)}) copy-start(f32[1024]{0:T(1024)} %param.23) | copy-start | bytes 12292
  2.7 15.6 %all-to-all-start = ((bf16[8,104,128]{2,1,0:T(8,128)(2,1)}), bf16[8,104,128]{2,1,0:T(8,128)(2,1)S(1)}, u32[]{:S(2)}, u32[]{:S(2)}) async-start(bf16[8,104,128]{2,1,0:T(8,128)(2,1)} %shard_map.158), calls=%async_computation | async-start | bytes 425984 | tf_op jit(solution)/shard_map/all_to_all | solution.py:359
  10.1 0.8 %copy-start.1 = (bf16[8,1024]{1,0:T(8,128)(2,1)S(1)}, bf16[8,1024]{1,0:T(8,128)(2,1)}, u32[]{:S(2)}) copy-start(bf16[8,1024]{1,0:T(8,128)(2,1)} %param.19) | copy-start | bytes 49156
  10.2 0.7 %copy-start.4 = (s32[256,4]{0,1:T(4,128)S(1)}, s32[256,4]{0,1:T(4,128)}, u32[]{:S(2)}) copy-start(s32[256,4]{0,1:T(4,128)} %param.29) | copy-start | bytes 12292
  10.9 0.7 %copy-start.5 = (f32[256]{0:T(256)S(1)}, f32[256]{0:T(256)}, u32[]{:S(2)}) copy-start(f32[256]{0:T(256)} %param.26) | copy-start | bytes 3076
  10.9 0.7 %copy-start.6 = (f32[256]{0:T(256)S(1)}, f32[256]{0:T(256)}, u32[]{:S(2)}) copy-start(f32[256]{0:T(256)} %param.25) | copy-start | bytes 3076

commit v7 on v6

--- a/solution.py
+++ b/solution.py
@@ -45,6 +45,23 @@
         )
         at += count
     return total
+
+
+def position(device, member, count):
+    place = jnp.where(device < count // 2, 2 * device, 2 * (count - 1 - device) + 1)
+    place = jnp.where(lax.rem(member, 2) == 1, count - 1 - place, place)
+    return jnp.where(lax.rem(member // 2, 2) == 1, lax.rem(place + count // 2, count), place)
+
+
+def exchange_groups(count, members):
+    ends = [x for pair in zip(range(count // 2), range(count - 1, count // 2 - 1, -1), strict=True) for x in pair]
+    groups = []
+    for member in range(members):
+        order = ends[::-1] if member % 2 else ends
+        if member // 2 % 2:
+            order = order[count // 2 :] + order[: count // 2]
+        groups.append([device * members + member for device in order])
+    return groups
 
 
 def pack_kernel(basin_local, *refs):
@@ -77,6 +94,7 @@
     owners = LANES // basin_local
     lane = lax.broadcasted_iota(jnp.int32, (1, LANES), 1)
     mine = lane // basin_local == lax.rem(lax.axis_index("basin"), owners)
+    mine_member = lax.axis_index("member")
     for member in range(members):
         tiles = forcing[:, member, :]
         first = tiles[:, :LANES]
@@ -86,10 +104,10 @@
         rows = common + pieces(jnp.where(mine, own_flow, 0.0))
         extras = jnp.concatenate(rows, axis=0).astype(jnp.bfloat16)
         for group in range(groups):
-            device = member * groups + group
-            send[device, :tile_local, :] = first
-            send[device, tile_local : tile_local + half, :] = second
-            send[device, tile_local + half :, :] = extras
+            place = position(member * groups + group, mine_member, send.shape[0])
+            send[place, :tile_local, :] = first
+            send[place, tile_local : tile_local + half, :] = second
+            send[place, tile_local + half :, :] = extras
 
 
 def encode(values):
@@ -152,8 +170,11 @@
     inputs = total.astype(jnp.bfloat16)
 
     owners = rows // basin_local
-    flow = arrived[pl.ds(half * owners, owners), extra_at:, :].astype(jnp.float32)
-    flow = jnp.sum(flow, axis=0)
+    member = lax.axis_index("member")
+    flow = jnp.zeros((EXTRAS, rows), jnp.float32)
+    for owner in range(owners):
+        place = position(half * owners + owner, member, devices)
+        flow = flow + arrived[place, extra_at:, :].astype(jnp.float32)
     results = []
     b_encoder, b_decoder = small[0:1, : 4 * units], small[1:2, : 4 * units]
     w_input = small[INPUT_ROW : INPUT_ROW + FEAT, : 4 * units].astype(jnp.bfloat16)
@@ -356,7 +377,14 @@
         + [pltpu.SemaphoreType.DMA((len(operands),))],
         compiler_params=pltpu.CompilerParams(vmem_limit_bytes=60 << 20),
     )(*operands)
-    arrived = lax.all_to_all(send, "basin", split_axis=0, concat_axis=0, tiled=True)
+    arrived = lax.all_to_all(
+        send,
+        ("basin", "member"),
+        split_axis=0,
+        concat_axis=0,
+        tiled=True,
+        axis_index_groups=exchange_groups(part_count, lax.axis_size("member")),
+    )
     sources = min(part_count, 8)
     units = w_encoder.shape[0]
     scale = jnp.where(jnp.arange(4 * units) // units == 2, 1.0, 0.5).astype(jnp.float32)

time: 38.4 us -> 38.1 us (level)
  waiting for transfers between devices: 5.37 us -> 4.03 us
  blocking collectives: 10.4 us -> 11.3 us
    all_to_all x1, waiting for transfers between devices: 5.37 us -> 4.03 us  [on_device(): lax.all_to_all(send, ('basin', 'member'), split_axis=0, concat_axis=0, ti...]
    all_to_all x1, blocking collectives: 10.4 us -> 11.3 us  [on_device(): lax.all_to_all(copies, axes, split_axis=0, concat_axis=0, tiled=True)]
where the time goes in v7:
time: 38.1 us; the launch traced here: 37.7 us
  Pallas kernels  11.3 us (30%)
  blocking collectives  11.3 us (30%)
  starting transfers between devices  7.42 us (19%)
  waiting for transfers between devices  4.03 us (11%)
  local copies, waits for them, and re-layouts  1.39 us (4%)
  other arithmetic  1.35 us (4%)
  between operations  0.83 us (2%)
    all_to_all x1, blocking collectives, on_device(): lax.all_to_all(copies, axes, split_axis=0, concat_axis=0, tiled=True)  11.3 us
    all_to_all x1, starting transfers between devices, on_device(): lax.all_to_all(send, ('basin', 'member'), split_axis=0, concat_axis=0, ti...  7.42 us
    pallas_call x1, Pallas kernels, on_device(): pl.pallas_call(functools.partial(lstm_kernel, (hour_feat, tile_local, bas...  6.96 us
    all_to_all x1, waiting for transfers between devices, on_device(): lax.all_to_all(send, ('basin', 'member'), split_axis=0, concat_axis=0, ti...  4.03 us
    pallas_call x1, Pallas kernels, on_device(): pl.pallas_call(functools.partial(route_kernel, mem_local, basin_local, re...  2.38 us
    pallas_call x1, Pallas kernels, on_device(): pl.pallas_call(functools.partial(pack_kernel, basin_local), out_shape=jax...  1.97 us
    unnamed x18, local copies, waits for them, and re-layouts  1.37 us
    convert_element_type x1, other arithmetic, on_device(): w_decoder = (w_decoder * scale).astype(jnp.bfloat16)  1.28 us
  transfers between devices with their start and end apart: 1, of which 1 were waited for; matrix products, arithmetic and copies ran while one was open for 4% of the time, Pallas kernels for 0%

profile of v7, /device:TPU:0, one launch (start us, length us, event | category | flops | bytes accessed | tf_op | source)
XLA Modules:
  0.0 37.7 jit_solution(11589408320753604879)
XLA Ops:
  0.6 0.0 copy-start
  0.6 2.0 %shard_map.158 = bf16[8,104,128]{2,1,0:T(8,128)(2,1)} custom-call(bf16[64,4,192]{2,1,0:T(4,128)(2,1)} %refs_0_.1, f32[2,64]{1,0:T(2,128)} %bitcast.20, s32[2,64]{1,0:T(2,128)} %bitcast.21, s32[2,64]{1,0:T(2,128)} %bitcast.22, f32[4,32]{1,0:T(4,128)} %bitcast.19), custom_call_target="tpu_custom_call" | custom-call | tf_op jit(solution)/shard_map/pallas_call | solution.py:369
  2.6 0.0 copy-start.8
  2.6 0.0 copy-start.7
  2.6 0.0 copy-start.2
  2.7 0.0 copy-start.3
  2.7 7.4 %all-to-all-start = ((bf16[8,104,128]{2,1,0:T(8,128)(2,1)}), bf16[8,104,128]{2,1,0:T(8,128)(2,1)S(1)}, u32[]{:S(2)}, u32[]{:S(2)}) async-start(bf16[8,104,128]{2,1,0:T(8,128)(2,1)} %shard_map.158), calls=%async_computation | async-start | bytes 425984 | tf_op jit(solution)/shard_map/all_to_all | solution.py:380
  10.1 0.0 copy-start.1
  10.1 0.0 copy-done.8
  10.1 0.0 copy-done.7
  10.2 0.0 copy-done.2
  10.2 0.0 copy-done.3
  10.2 0.0 copy-start.4
  10.2 0.7 %copy-done.4 = s32[256,4]{0,1:T(4,128)S(1)} copy-done((s32[256,4]{0,1:T(4,128)S(1)}, s32[256,4]{0,1:T(4,128)}, u32[]{:S(2)}) %copy-start.4) | copy-done | bytes 4120
  10.9 0.0 copy-done.1
  10.9 0.0 copy-start.5
  10.9 0.0 copy-start.6
  10.9 0.6 %copy-done.5 = f32[256]{0:T(256)S(1)} copy-done((f32[256]{0:T(256)S(1)}, f32[256]{0:T(256)}, u32[]{:S(2)}) %copy-start.5) | copy-done | bytes 1048
  11.6 0.0 copy-done.6
  11.6 0.0 copy-done
  11.6 1.3 %multiply_convert_fusion = (bf16[256,1024]{1,0:T(8,128)(2,1)S(1)}, bf16[256,1024]{1,0:T(8,128)(2,1)S(1)}) fusion(bf16[256,1024]{1,0:T(8,128)(2,1)S(1)} %copy-done, f32[1024]{0:T(1024)S(1)} %fusion.4, bf16[256,1024]{1,0:T(8,128)(2,1)} %param.20), kind=kLoop, calls=%fused_computation | loop fusion | flops 1572864 | bytes 2101248 | tf_op jit(solution)/shard_map/convert_element_type | solution.py:395
  12.9 4.0 %all-to-all-done.arrived = bf16[8,104,128]{2,1,0:T(8,128)(2,1)S(1)} async-done(((bf16[8,104,128]{2,1,0:T(8,128)(2,1)}), bf16[8,104,128]{2,1,0:T(8,128)(2,1)S(1)}, u32[]{:S(2)}, u32[]{:S(2)}) %all-to-all-start) | async-done | bytes 213024 | tf_op jit(solution)/shard_map/all_to_all | solution.py:380
  16.9 7.0 %shard_map.159 = f32[8,128]{1,0:T(8,128)S(1)} custom-call(bf16[8,104,128]{2,1,0:T(8,128)(2,1)S(1)} %all-to-all-done.arrived, f32[24,1024]{1,0:T(8,128)S(1)} %pad_add_fusion.small, bf16[256,1024]{1,0:T(8,128)(2,1)S(1)} %get-tuple-element.7.w_encoder, bf16[256,1024]{1,0:T(8,128)(2,1)S(1)} %get-tuple-element.6.w_decoder), custom_call_target="tpu_custom_call" | custom-call | tf_op jit(solution)/shard_map/pallas_call | solution.py:396
  23.9 11.3 %all_to_all.10 = f16[32,8,128]{2,1,0:T(8,128)(2,1)S(1)} all-to-all(f16[32,8,128]{2,1,0:T(8,128)(2,1)S(1)} %broadcast_in_dim.18), channel_id=1, replica_groups=mesh['basin'=8,'member'=4] {'member','basin'}, dimensions={0} | all-to-all | bytes 131072 | tf_op jit(solution)/shard_map/all_to_all | solution.py:406
  35.3 2.4 %shard_map.160 = (f32[6,4,32]{2,1,0:T(4,128)}, f32[6,32]{1,0:T(8,128)}) custom-call(f32[256,128]{1,0:T(8,128)S(1)} %bitcast_convert_fusion.gathered, f32[24,1024]{1,0:T(8,128)S(1)} %pad_add_fusion.small), custom_call_target="tpu_custom_call" | custom-call | tf_op jit(solution)/shard_map/pallas_call | solution.py:410
  (12 shorter events, 0.1 us)
Async XLA Ops:
  0.6 11.0 %copy-start = (bf16[256,1024]{1,0:T(8,128)(2,1)S(1)}, bf16[256,1024]{1,0:T(8,128)(2,1)}, u32[]{:S(2)}) copy-start(bf16[256,1024]{1,0:T(8,128)(2,1)} %param.22) | copy-start | bytes 1572868
  2.6 7.5 %copy-start.8 = (bf16[256]{0:T(256)(128)(2,1)S(1)}, bf16[256]{0:T(256)(128)(2,1)}, u32[]{:S(2)}) copy-start(bf16[256]{0:T(256)(128)(2,1)} %param.24) | copy-start | bytes 1540
  2.6 7.5 %copy-start.7 = (s32[256]{0:T(256)S(1)}, s32[256]{0:T(256)}, u32[]{:S(2)}) copy-start(s32[256]{0:T(256)} %param.28) | copy-start | bytes 3076
  2.6 7.5 %copy-start.2 = (f32[1024]{0:T(1024)S(1)}, f32[1024]{0:T(1024)}, u32[]{:S(2)}) copy-start(f32[1024]{0:T(1024)} %param.21) | copy-start | bytes 12292
  2.7 7.5 %copy-start.3 = (f32[1024]{0:T(1024)S(1)}, f32[1024]{0:T(1024)}, u32[]{:S(2)}) copy-start(f32[1024]{0:T(1024)} %param.23) | copy-start | bytes 12292
  2.7 14.3 %all-to-all-start = ((bf16[8,104,128]{2,1,0:T(8,128)(2,1)}), bf16[8,104,128]{2,1,0:T(8,128)(2,1)S(1)}, u32[]{:S(2)}, u32[]{:S(2)}) async-start(bf16[8,104,128]{2,1,0:T(8,128)(2,1)} %shard_map.158), calls=%async_computation | async-start | bytes 425984 | tf_op jit(solution)/shard_map/all_to_all | solution.py:380
  10.1 0.8 %copy-start.1 = (bf16[8,1024]{1,0:T(8,128)(2,1)S(1)}, bf16[8,1024]{1,0:T(8,128)(2,1)}, u32[]{:S(2)}) copy-start(bf16[8,1024]{1,0:T(8,128)(2,1)} %param.19) | copy-start | bytes 49156
  10.2 0.7 %copy-start.4 = (s32[256,4]{0,1:T(4,128)S(1)}, s32[256,4]{0,1:T(4,128)}, u32[]{:S(2)}) copy-start(s32[256,4]{0,1:T(4,128)} %param.29) | copy-start | bytes 12292
  10.9 0.7 %copy-start.5 = (f32[256]{0:T(256)S(1)}, f32[256]{0:T(256)}, u32[]{:S(2)}) copy-start(f32[256]{0:T(256)} %param.26) | copy-start | bytes 3076
  10.9 0.7 %copy-start.6 = (f32[256]{0:T(256)S(1)}, f32[256]{0:T(256)}, u32[]{:S(2)}) copy-start(f32[256]{0:T(256)} %param.25) | copy-start | bytes 3076

commit v8 on v7

--- a/solution.py
+++ b/solution.py
@@ -19,6 +19,12 @@
 CARRIED = jnp.float16
 HALF_STEP = 2.0**11
 INPUT_ROW = 16
+ORDERS = (
+    (7, 2, 5, 4, 6, 0, 1, 3),
+    (5, 3, 2, 6, 1, 7, 0, 4),
+    (7, 2, 1, 6, 5, 0, 4, 3),
+    (5, 7, 3, 0, 4, 6, 2, 1),
+)
 
 dot = functools.partial(jnp.dot, preferred_element_type=jnp.float32)
 
@@ -48,6 +54,14 @@
 
 
 def position(device, member, count):
+    if (lax.axis_size("member"), count) == (len(ORDERS), len(ORDERS[0])):
+        place = jnp.int32(0)
+        for index, order in enumerate(ORDERS):
+            here = jnp.int32(0)
+            for at, named in enumerate(order):
+                here = jnp.where(device == named, at, here)
+            place = jnp.where(member == index, here, place)
+        return place
     place = jnp.where(device < count // 2, 2 * device, 2 * (count - 1 - device) + 1)
     place = jnp.where(lax.rem(member, 2) == 1, count - 1 - place, place)
     return jnp.where(lax.rem(member // 2, 2) == 1, lax.rem(place + count // 2, count), place)
@@ -60,6 +74,8 @@
         order = ends[::-1] if member % 2 else ends
         if member // 2 % 2:
             order = order[count // 2 :] + order[: count // 2]
+        if (members, count) == (len(ORDERS), len(ORDERS[0])):
+            order = ORDERS[member]
         groups.append([device * members + member for device in order])
     return groups
 

time: 38.1 us -> 37.7 us (0.990)
  waiting for transfers between devices: 4.03 us -> 1.65 us
  starting transfers between devices: 7.42 us -> 9.47 us
    all_to_all x1, waiting for transfers between devices: 4.03 us -> 1.65 us  [on_device(): lax.all_to_all(send, ('basin', 'member'), split_axis=0, concat_axis=0, ti...]
    all_to_all x1, starting transfers between devices: 7.42 us -> 9.47 us  [on_device(): lax.all_to_all(send, ('basin', 'member'), split_axis=0, concat_axis=0, ti...]
where the time goes in v8:
time: 37.7 us; the launch traced here: 37.3 us
  Pallas kernels  11.3 us (30%)
  blocking collectives  11.3 us (30%)
  starting transfers between devices  9.47 us (25%)
  waiting for transfers between devices  1.65 us (4%)
  local copies, waits for them, and re-layouts  1.39 us (4%)
  other arithmetic  1.35 us (4%)
  between operations  0.82 us (2%)
    all_to_all x1, blocking collectives, on_device(): lax.all_to_all(copies, axes, split_axis=0, concat_axis=0, tiled=True)  11.3 us
    all_to_all x1, starting transfers between devices, on_device(): lax.all_to_all(send, ('basin', 'member'), split_axis=0, concat_axis=0, ti...  9.47 us
    pallas_call x1, Pallas kernels, on_device(): pl.pallas_call(functools.partial(lstm_kernel, (hour_feat, tile_local, bas...  6.96 us
    pallas_call x1, Pallas kernels, on_device(): pl.pallas_call(functools.partial(route_kernel, mem_local, basin_local, re...  2.38 us
    pallas_call x1, Pallas kernels, on_device(): pl.pallas_call(functools.partial(pack_kernel, basin_local), out_shape=jax...  1.96 us
    all_to_all x1, waiting for transfers between devices, on_device(): lax.all_to_all(send, ('basin', 'member'), split_axis=0, concat_axis=0, ti...  1.65 us
    unnamed x18, local copies, waits for them, and re-layouts  1.37 us
    convert_element_type x1, other arithmetic, on_device(): w_decoder = (w_decoder * scale).astype(jnp.bfloat16)  1.28 us
  transfers between devices with their start and end apart: 1, of which 1 were waited for; matrix products, arithmetic and copies ran while one was open for 4% of the time, Pallas kernels for 0%

profile of v8, /device:TPU:0, one launch (start us, length us, event | category | flops | bytes accessed | tf_op | source)
XLA Modules:
  0.0 37.3 jit_solution(15640876015207395210)
XLA Ops:
  0.6 0.0 copy-start
  0.6 2.0 %shard_map.158 = bf16[8,104,128]{2,1,0:T(8,128)(2,1)} custom-call(bf16[64,4,192]{2,1,0:T(4,128)(2,1)} %refs_0_.1, f32[2,64]{1,0:T(2,128)} %bitcast.20, s32[2,64]{1,0:T(2,128)} %bitcast.21, s32[2,64]{1,0:T(2,128)} %bitcast.22, f32[4,32]{1,0:T(4,128)} %bitcast.19), custom_call_target="tpu_custom_call" | custom-call | tf_op jit(solution)/shard_map/pallas_call | solution.py:385
  2.6 0.0 copy-start.8
  2.6 0.0 copy-start.7
  2.6 0.0 copy-start.2
  2.6 0.0 copy-start.3
  2.7 9.5 %all-to-all-start = ((bf16[8,104,128]{2,1,0:T(8,128)(2,1)}), bf16[8,104,128]{2,1,0:T(8,128)(2,1)S(1)}, u32[]{:S(2)}, u32[]{:S(2)}) async-start(bf16[8,104,128]{2,1,0:T(8,128)(2,1)} %shard_map.158), calls=%async_computation | async-start | bytes 425984 | tf_op jit(solution)/shard_map/all_to_all | solution.py:396
  12.1 0.0 copy-start.1
  12.1 0.0 copy-done.8
  12.2 0.0 copy-done.7
  12.2 0.0 copy-done.2
  12.2 0.0 copy-done.3
  12.2 0.0 copy-start.4
  12.2 0.7 %copy-done.4 = s32[256,4]{0,1:T(4,128)S(1)} copy-done((s32[256,4]{0,1:T(4,128)S(1)}, s32[256,4]{0,1:T(4,128)}, u32[]{:S(2)}) %copy-start.4) | copy-done | bytes 4120
  12.9 0.0 copy-done.1
  12.9 0.0 copy-start.5
  12.9 0.0 copy-start.6
  13.0 0.6 %copy-done.5 = f32[256]{0:T(256)S(1)} copy-done((f32[256]{0:T(256)S(1)}, f32[256]{0:T(256)}, u32[]{:S(2)}) %copy-start.5) | copy-done | bytes 1048
  13.6 0.0 copy-done.6
  13.6 0.0 copy-done
  13.7 1.3 %multiply_convert_fusion = (bf16[256,1024]{1,0:T(8,128)(2,1)S(1)}, bf16[256,1024]{1,0:T(8,128)(2,1)S(1)}) fusion(bf16[256,1024]{1,0:T(8,128)(2,1)S(1)} %copy-done, f32[1024]{0:T(1024)S(1)} %fusion.4, bf16[256,1024]{1,0:T(8,128)(2,1)} %param.20), kind=kLoop, calls=%fused_computation | loop fusion | flops 1572864 | bytes 2101248 | tf_op jit(solution)/shard_map/convert_element_type | solution.py:411
  14.9 1.7 %all-to-all-done.arrived = bf16[8,104,128]{2,1,0:T(8,128)(2,1)S(1)} async-done(((bf16[8,104,128]{2,1,0:T(8,128)(2,1)}), bf16[8,104,128]{2,1,0:T(8,128)(2,1)S(1)}, u32[]{:S(2)}, u32[]{:S(2)}) %all-to-all-start) | async-done | bytes 213024 | tf_op jit(solution)/shard_map/all_to_all | solution.py:396
  16.6 7.0 %shard_map.159 = f32[8,128]{1,0:T(8,128)S(1)} custom-call(bf16[8,104,128]{2,1,0:T(8,128)(2,1)S(1)} %all-to-all-done.arrived, f32[24,1024]{1,0:T(8,128)S(1)} %pad_add_fusion.small, bf16[256,1024]{1,0:T(8,128)(2,1)S(1)} %get-tuple-element.7.w_encoder, bf16[256,1024]{1,0:T(8,128)(2,1)S(1)} %get-tuple-element.6.w_decoder), custom_call_target="tpu_custom_call" | custom-call | tf_op jit(solution)/shard_map/pallas_call | solution.py:412
  23.6 11.3 %all_to_all.10 = f16[32,8,128]{2,1,0:T(8,128)(2,1)S(1)} all-to-all(f16[32,8,128]{2,1,0:T(8,128)(2,1)S(1)} %broadcast_in_dim.18), channel_id=1, replica_groups=mesh['basin'=8,'member'=4] {'member','basin'}, dimensions={0} | all-to-all | bytes 131072 | tf_op jit(solution)/shard_map/all_to_all | solution.py:422
  35.0 2.4 %shard_map.160 = (f32[6,4,32]{2,1,0:T(4,128)}, f32[6,32]{1,0:T(8,128)}) custom-call(f32[256,128]{1,0:T(8,128)S(1)} %bitcast_convert_fusion.gathered, f32[24,1024]{1,0:T(8,128)S(1)} %pad_add_fusion.small), custom_call_target="tpu_custom_call" | custom-call | tf_op jit(solution)/shard_map/pallas_call | solution.py:426
  (12 shorter events, 0.1 us)
Async XLA Ops:
  0.6 13.0 %copy-start = (bf16[256,1024]{1,0:T(8,128)(2,1)S(1)}, bf16[256,1024]{1,0:T(8,128)(2,1)}, u32[]{:S(2)}) copy-start(bf16[256,1024]{1,0:T(8,128)(2,1)} %param.22) | copy-start | bytes 1572868
  2.6 9.5 %copy-start.8 = (bf16[256]{0:T(256)(128)(2,1)S(1)}, bf16[256]{0:T(256)(128)(2,1)}, u32[]{:S(2)}) copy-start(bf16[256]{0:T(256)(128)(2,1)} %param.24) | copy-start | bytes 1540
  2.6 9.5 %copy-start.7 = (s32[256]{0:T(256)S(1)}, s32[256]{0:T(256)}, u32[]{:S(2)}) copy-start(s32[256]{0:T(256)} %param.28) | copy-start | bytes 3076
  2.6 9.6 %copy-start.2 = (f32[1024]{0:T(1024)S(1)}, f32[1024]{0:T(1024)}, u32[]{:S(2)}) copy-start(f32[1024]{0:T(1024)} %param.21) | copy-start | bytes 12292
  2.6 9.6 %copy-start.3 = (f32[1024]{0:T(1024)S(1)}, f32[1024]{0:T(1024)}, u32[]{:S(2)}) copy-start(f32[1024]{0:T(1024)} %param.23) | copy-start | bytes 12292
  2.7 13.9 %all-to-all-start = ((bf16[8,104,128]{2,1,0:T(8,128)(2,1)}), bf16[8,104,128]{2,1,0:T(8,128)(2,1)S(1)}, u32[]{:S(2)}, u32[]{:S(2)}) async-start(bf16[8,104,128]{2,1,0:T(8,128)(2,1)} %shard_map.158), calls=%async_computation | async-start | bytes 425984 | tf_op jit(solution)/shard_map/all_to_all | solution.py:396
  12.1 0.8 %copy-start.1 = (bf16[8,1024]{1,0:T(8,128)(2,1)S(1)}, bf16[8,1024]{1,0:T(8,128)(2,1)}, u32[]{:S(2)}) copy-start(bf16[8,1024]{1,0:T(8,128)(2,1)} %param.19) | copy-start | bytes 49156
  12.2 0.7 %copy-start.4 = (s32[256,4]{0,1:T(4,128)S(1)}, s32[256,4]{0,1:T(4,128)}, u32[]{:S(2)}) copy-start(s32[256,4]{0,1:T(4,128)} %param.29) | copy-start | bytes 12292
  12.9 0.7 %copy-start.5 = (f32[256]{0:T(256)S(1)}, f32[256]{0:T(256)}, u32[]{:S(2)}) copy-start(f32[256]{0:T(256)} %param.26) | copy-start | bytes 3076
  12.9 0.7 %copy-start.6 = (f32[256]{0:T(256)S(1)}, f32[256]{0:T(256)}, u32[]{:S(2)}) copy-start(f32[256]{0:T(256)} %param.25) | copy-start | bytes 3076

commit v9 on v8

--- a/solution.py
+++ b/solution.py
@@ -19,12 +19,7 @@
 CARRIED = jnp.float16
 HALF_STEP = 2.0**11
 INPUT_ROW = 16
-ORDERS = (
-    (7, 2, 5, 4, 6, 0, 1, 3),
-    (5, 3, 2, 6, 1, 7, 0, 4),
-    (7, 2, 1, 6, 5, 0, 4, 3),
-    (5, 7, 3, 0, 4, 6, 2, 1),
-)
+ORDERS = ((7, 2, 5, 4, 6, 0, 1, 3), (5, 3, 2, 6, 1, 7, 0, 4), (7, 2, 5, 4, 6, 0, 1, 3), (5, 3, 2, 6, 1, 7, 0, 4))
 
 dot = functools.partial(jnp.dot, preferred_element_type=jnp.float32)
 

time: 37.7 us -> 37.4 us (level)
  no operation moved by 1% of the time
where the time goes in v9:
time: 37.4 us; the launch traced here: 37.1 us
  Pallas kernels  11.3 us (30%)
  blocking collectives  11.1 us (30%)
  starting transfers between devices  9.47 us (25%)
  waiting for transfers between devices  1.65 us (4%)
  local copies, waits for them, and re-layouts  1.39 us (4%)
  other arithmetic  1.35 us (4%)
  between operations  0.82 us (2%)
    all_to_all x1, blocking collectives, on_device(): lax.all_to_all(copies, axes, split_axis=0, concat_axis=0, tiled=True)  11.1 us
    all_to_all x1, starting transfers between devices, on_device(): lax.all_to_all(send, ('basin', 'member'), split_axis=0, concat_axis=0, ti...  9.47 us
    pallas_call x1, Pallas kernels, on_device(): pl.pallas_call(functools.partial(lstm_kernel, (hour_feat, tile_local, bas...  6.96 us
    pallas_call x1, Pallas kernels, on_device(): pl.pallas_call(functools.partial(route_kernel, mem_local, basin_local, re...  2.38 us
    pallas_call x1, Pallas kernels, on_device(): pl.pallas_call(functools.partial(pack_kernel, basin_local), out_shape=jax...  1.96 us
    all_to_all x1, waiting for transfers between devices, on_device(): lax.all_to_all(send, ('basin', 'member'), split_axis=0, concat_axis=0, ti...  1.65 us
    unnamed x18, local copies, waits for them, and re-layouts  1.37 us
    convert_element_type x1, other arithmetic, on_device(): w_decoder = (w_decoder * scale).astype(jnp.bfloat16)  1.28 us
  transfers between devices with their start and end apart: 1, of which 1 were waited for; matrix products, arithmetic and copies ran while one was open for 4% of the time, Pallas kernels for 0%

profile of v9, /device:TPU:0, one launch (start us, length us, event | category | flops | bytes accessed | tf_op | source)
XLA Modules:
  0.0 37.1 jit_solution(4377894098120603532)
XLA Ops:
  0.6 0.0 copy-start
  0.6 2.0 %shard_map.158 = bf16[8,104,128]{2,1,0:T(8,128)(2,1)} custom-call(bf16[64,4,192]{2,1,0:T(4,128)(2,1)} %refs_0_.1, f32[2,64]{1,0:T(2,128)} %bitcast.20, s32[2,64]{1,0:T(2,128)} %bitcast.21, s32[2,64]{1,0:T(2,128)} %bitcast.22, f32[4,32]{1,0:T(4,128)} %bitcast.19), custom_call_target="tpu_custom_call" | custom-call | tf_op jit(solution)/shard_map/pallas_call | solution.py:380
  2.6 0.0 copy-start.8
  2.6 0.0 copy-start.7
  2.6 0.0 copy-start.2
  2.6 0.0 copy-start.3
  2.7 9.5 %all-to-all-start = ((bf16[8,104,128]{2,1,0:T(8,128)(2,1)}), bf16[8,104,128]{2,1,0:T(8,128)(2,1)S(1)}, u32[]{:S(2)}, u32[]{:S(2)}) async-start(bf16[8,104,128]{2,1,0:T(8,128)(2,1)} %shard_map.158), calls=%async_computation | async-start | bytes 425984 | tf_op jit(solution)/shard_map/all_to_all | solution.py:391
  12.1 0.0 copy-start.1
  12.1 0.0 copy-done.8
  12.2 0.0 copy-done.7
  12.2 0.0 copy-done.2
  12.2 0.0 copy-done.3
  12.2 0.0 copy-start.4
  12.2 0.7 %copy-done.4 = s32[256,4]{0,1:T(4,128)S(1)} copy-done((s32[256,4]{0,1:T(4,128)S(1)}, s32[256,4]{0,1:T(4,128)}, u32[]{:S(2)}) %copy-start.4) | copy-done | bytes 4120
  12.9 0.0 copy-done.1
  12.9 0.0 copy-start.5
  12.9 0.0 copy-start.6
  13.0 0.6 %copy-done.5 = f32[256]{0:T(256)S(1)} copy-done((f32[256]{0:T(256)S(1)}, f32[256]{0:T(256)}, u32[]{:S(2)}) %copy-start.5) | copy-done | bytes 1048
  13.6 0.0 copy-done.6
  13.6 0.0 copy-done
  13.7 1.3 %multiply_convert_fusion = (bf16[256,1024]{1,0:T(8,128)(2,1)S(1)}, bf16[256,1024]{1,0:T(8,128)(2,1)S(1)}) fusion(bf16[256,1024]{1,0:T(8,128)(2,1)S(1)} %copy-done, f32[1024]{0:T(1024)S(1)} %fusion.4, bf16[256,1024]{1,0:T(8,128)(2,1)} %param.20), kind=kLoop, calls=%fused_computation | loop fusion | flops 1572864 | bytes 2101248 | tf_op jit(solution)/shard_map/convert_element_type | solution.py:406
  14.9 1.7 %all-to-all-done.arrived = bf16[8,104,128]{2,1,0:T(8,128)(2,1)S(1)} async-done(((bf16[8,104,128]{2,1,0:T(8,128)(2,1)}), bf16[8,104,128]{2,1,0:T(8,128)(2,1)S(1)}, u32[]{:S(2)}, u32[]{:S(2)}) %all-to-all-start) | async-done | bytes 213024 | tf_op jit(solution)/shard_map/all_to_all | solution.py:391
  16.6 7.0 %shard_map.159 = f32[8,128]{1,0:T(8,128)S(1)} custom-call(bf16[8,104,128]{2,1,0:T(8,128)(2,1)S(1)} %all-to-all-done.arrived, f32[24,1024]{1,0:T(8,128)S(1)} %pad_add_fusion.small, bf16[256,1024]{1,0:T(8,128)(2,1)S(1)} %get-tuple-element.7.w_encoder, bf16[256,1024]{1,0:T(8,128)(2,1)S(1)} %get-tuple-element.6.w_decoder), custom_call_target="tpu_custom_call" | custom-call | tf_op jit(solution)/shard_map/pallas_call | solution.py:407
  23.6 11.1 %all_to_all.10 = f16[32,8,128]{2,1,0:T(8,128)(2,1)S(1)} all-to-all(f16[32,8,128]{2,1,0:T(8,128)(2,1)S(1)} %broadcast_in_dim.18), channel_id=1, replica_groups=mesh['basin'=8,'member'=4] {'member','basin'}, dimensions={0} | all-to-all | bytes 131072 | tf_op jit(solution)/shard_map/all_to_all | solution.py:417
  34.7 2.4 %shard_map.160 = (f32[6,4,32]{2,1,0:T(4,128)}, f32[6,32]{1,0:T(8,128)}) custom-call(f32[256,128]{1,0:T(8,128)S(1)} %bitcast_convert_fusion.gathered, f32[24,1024]{1,0:T(8,128)S(1)} %pad_add_fusion.small), custom_call_target="tpu_custom_call" | custom-call | tf_op jit(solution)/shard_map/pallas_call | solution.py:421
  (12 shorter events, 0.1 us)
Async XLA Ops:
  0.6 13.0 %copy-start = (bf16[256,1024]{1,0:T(8,128)(2,1)S(1)}, bf16[256,1024]{1,0:T(8,128)(2,1)}, u32[]{:S(2)}) copy-start(bf16[256,1024]{1,0:T(8,128)(2,1)} %param.22) | copy-start | bytes 1572868
  2.6 9.5 %copy-start.8 = (bf16[256]{0:T(256)(128)(2,1)S(1)}, bf16[256]{0:T(256)(128)(2,1)}, u32[]{:S(2)}) copy-start(bf16[256]{0:T(256)(128)(2,1)} %param.24) | copy-start | bytes 1540
  2.6 9.5 %copy-start.7 = (s32[256]{0:T(256)S(1)}, s32[256]{0:T(256)}, u32[]{:S(2)}) copy-start(s32[256]{0:T(256)} %param.28) | copy-start | bytes 3076
  2.6 9.6 %copy-start.2 = (f32[1024]{0:T(1024)S(1)}, f32[1024]{0:T(1024)}, u32[]{:S(2)}) copy-start(f32[1024]{0:T(1024)} %param.21) | copy-start | bytes 12292
  2.6 9.6 %copy-start.3 = (f32[1024]{0:T(1024)S(1)}, f32[1024]{0:T(1024)}, u32[]{:S(2)}) copy-start(f32[1024]{0:T(1024)} %param.23) | copy-start | bytes 12292
  2.7 13.9 %all-to-all-start = ((bf16[8,104,128]{2,1,0:T(8,128)(2,1)}), bf16[8,104,128]{2,1,0:T(8,128)(2,1)S(1)}, u32[]{:S(2)}, u32[]{:S(2)}) async-start(bf16[8,104,128]{2,1,0:T(8,128)(2,1)} %shard_map.158), calls=%async_computation | async-start | bytes 425984 | tf_op jit(solution)/shard_map/all_to_all | solution.py:391
  12.1 0.8 %copy-start.1 = (bf16[8,1024]{1,0:T(8,128)(2,1)S(1)}, bf16[8,1024]{1,0:T(8,128)(2,1)}, u32[]{:S(2)}) copy-start(bf16[8,1024]{1,0:T(8,128)(2,1)} %param.19) | copy-start | bytes 49156
  12.2 0.7 %copy-start.4 = (s32[256,4]{0,1:T(4,128)S(1)}, s32[256,4]{0,1:T(4,128)}, u32[]{:S(2)}) copy-start(s32[256,4]{0,1:T(4,128)} %param.29) | copy-start | bytes 12292
  12.9 0.7 %copy-start.5 = (f32[256]{0:T(256)S(1)}, f32[256]{0:T(256)}, u32[]{:S(2)}) copy-start(f32[256]{0:T(256)} %param.26) | copy-start | bytes 3076
  12.9 0.7 %copy-start.6 = (f32[256]{0:T(256)S(1)}, f32[256]{0:T(256)}, u32[]{:S(2)}) copy-start(f32[256]{0:T(256)} %param.25) | copy-start | bytes 3076
